TPU v7x, 512 devices: a whole 4x8x8 slice. The times are simulated.
512 devices in a mesh: shard: 128 (over z, y, core), tile: 4 (over x).
Axes of the slice: x: 4, y: 8, z: 8, core: 2. Of those that a mesh axis runs over, the one named last changes fastest.
Arguments:
- embeddings: bfloat16 [262144, 768], P(('shard', 'tile'))
- cluster: int32 [262144], P(('shard', 'tile')), may hold values from 0 to 15
- home: int32 [262144], P(('shard', 'tile')), may hold values from 0 to 127, as said below
Outputs:
- density: float32 [262144], P(('shard', 'tile'))
Inputs may be any that keep to these rules, and one draw needn't show every extreme that they name: `home`: among the rows of one device at most 8 name one owner, and in every draw some owner is named exactly that often by the rows of every device.
All inputs are finite; a program needn't handle non-finite values.
Results may differ from a plain program's by a relative error of at most 0.0045.
Values may be sent and summed in bfloat16 or wider, within the bound.
A program may use at most 64 MiB of HBM per device.

v0:
```python
import math

import jax
import jax.numpy as jnp
from jax import lax
from jax.sharding import PartitionSpec as P


def pair_sums(query_rows, query_ids, key_rows, key_ids):
    key_count = key_rows.shape[0]
    block = math.gcd(512, key_count)
    key_blocks = key_rows.reshape(key_count // block, block, key_rows.shape[1])
    id_blocks = key_ids.reshape(key_count // block, block)

    def advance(accrued, element):
        key_part, key_labels = element
        scores = lax.dot_general(
            query_rows, key_part, (((1,), (1,)), ((), ())), preferred_element_type=jnp.float32
        )
        matched = (query_ids[:, None] == key_labels[None, :]) & (query_ids[:, None] >= 0)
        weights = jnp.where(matched, jnp.exp((scores - 1.0) * 10.0), 0.0)
        return (accrued + jnp.sum(weights, axis=1), None)

    initial = jnp.zeros((query_rows.shape[0],), jnp.float32)
    row_sums, col_sums = lax.scan(advance, initial, (key_blocks, id_blocks))
    return (row_sums, None)


def shards(embeddings, cluster, home):
    n_shard = lax.axis_size("shard")
    row_count = embeddings.shape[0]
    feature_count = embeddings.shape[1]
    capacity = 2 * row_count // n_shard
    values = embeddings.astype(jnp.float32)
    unit_rows = (
        values * lax.rsqrt(jnp.sum(values * values, axis=1, keepdims=True) + 1e-06)
    ).astype(jnp.bfloat16)
    row_iota = jnp.arange(row_count, dtype=jnp.int32)
    same_dest = home[:, None] == home[None, :]
    earlier = row_iota[None, :] < row_iota[:, None]
    position = jnp.sum((same_dest & earlier).astype(jnp.int32), axis=1)
    slot_index = home * capacity + position
    outgoing = (
        jnp.zeros((n_shard * capacity, feature_count), jnp.bfloat16).at[slot_index].set(unit_rows)
    )
    slot_ids = jnp.full((n_shard * capacity,), -1, jnp.int32).at[slot_index].set(cluster)
    arrived, arrived_ids = (
        lax.all_to_all(
            outgoing.reshape(n_shard, capacity, feature_count),
            "shard",
            split_axis=0,
            concat_axis=0,
            tiled=True,
        ),
        lax.all_to_all(
            slot_ids.reshape(n_shard, capacity), "shard", split_axis=0, concat_axis=0, tiled=True
        ),
    )
    arrived = arrived.reshape(n_shard * capacity, feature_count)
    arrived_ids = arrived_ids.reshape(n_shard * capacity)
    row_sums, unused = pair_sums(
        arrived,
        arrived_ids,
        lax.all_gather(arrived, "tile", axis=0, tiled=True),
        lax.all_gather(arrived_ids, "tile", axis=0, tiled=True),
    )
    returned = lax.all_to_all(
        row_sums.reshape(n_shard, capacity), "shard", split_axis=0, concat_axis=0, tiled=True
    )
    return returned.reshape(n_shard * capacity)[slot_index]


def solution(mesh):
    return jax.shard_map(
        shards,
        mesh=mesh,
        in_specs=(P(("shard", "tile"), None), P(("shard", "tile")), P(("shard", "tile"))),
        out_specs=P(("shard", "tile")),
        check_vma=False,
    )
```

profile of v0, /device:TPU:1, one launch (start us, length us, event | category | flops | bytes accessed | tf_op | source)
XLA Modules:
  0.0 197.4 jit_solution(17004455177187128594)
XLA Ops:
  6.5 0.0 all-gather.2.cloned.1.call-start
  6.5 1.0 convert_reduce_fusion
  7.5 0.7 compare_select_fusion
  8.2 1.4 fusion.4
  9.6 3.7 %scatter_custom_fusion.1 = bf16[1024,768]{1,0:T(8,128)(2,1)S(1)} fusion(s32[512]{0:T(512)S(1)} %compare_select_fusion, bf16[512,768]{1,0:T(8,128)(2,1)} %param.5, f32[512]{0:T(512)S(1)} %add_rsqrt_fusion, bf16[]{:T(256)} %constant.45.clone.1), kind=kCustom, calls=%fused_computation.18 | custom fusion | flops 1179648 | bytes 2361346 | tf_op jit(solution)/shard_map/scatter | solution.py:44
  13.3 59.6 %all_to_all.26 = bf16[128,8,768]{2,1,0:T(8,128)(2,1)} all-to-all(bf16[128,8,768]{2,1,0:T(8,128)(2,1)S(1)} %bitcast.29), channel_id=1, replica_groups=mesh['shard'=128,'tile'=4] {'shard'}, dimensions={0} | all-to-all | bytes 3145728 | tf_op jit(solution)/shard_map/all_to_all | solution.py:48
  72.8 0.0 copy-start
  72.8 0.0 all-gather.2.cloned.1.call-update
  72.9 2.7 %scatter_custom_fusion = s32[1024]{0:T(1024)S(1)} fusion(s32[512]{0:T(512)S(1)} %compare_select_fusion, s32[512]{0:T(512)} %param.6, s32[]{:T(128)} %constant.49.clone.1), kind=kCustom, calls=%fused_computation.24 | custom fusion | bytes 4608 | tf_op jit(solution)/shard_map/scatter | solution.py:46
  75.6 0.7 all_to_all.17
  76.3 7.5 %all-to-all-start = ((s32[128,1,8]{2,1,0:T(1,128)}), s32[128,1,8]{2,1,0:T(1,128)S(1)}, u32[]{:S(2)}, u32[]{:S(2)}) async-start(s32[128,1,8]{2,1,0:T(1,128)} %bitcast), calls=%async_computation | async-start | bytes 131072 | tf_op jit(solution)/shard_map/all_to_all | solution.py:55
  83.9 11.4 %all-to-all-done = s32[128,1,8]{2,1,0:T(1,128)S(1)} async-done(((s32[128,1,8]{2,1,0:T(1,128)}), s32[128,1,8]{2,1,0:T(1,128)S(1)}, u32[]{:S(2)}, u32[]{:S(2)}) %all-to-all-start) | async-done | bytes 4128 | tf_op jit(solution)/shard_map/all_to_all | solution.py:55
  95.3 0.0 copy-start.1
  95.3 0.6 broadcast.67
  95.9 0.8 reduce.6
  96.7 0.1 reshape.47
  96.8 10.4 %all_gather.6 = s32[4096]{0:T(1024)S(1)} all-gather(s32[1024]{0:T(1024)S(1)} %reshape.47), channel_id=1, replica_groups=mesh['shard'=128,'tile'=4] {'tile'}, dimensions={0}, use_global_device_ids=true | all-gather | bytes 20480 | tf_op jit(solution)/shard_map/all_gather | solution.py:65
  107.2 0.1 eq.59
  107.3 31.5 %all-gather.2.cloned.1.call-done = bf16[4096,768]{1,0:T(8,128)(2,1)} async-done(((bf16[1024,768]{1,0:T(8,128)(2,1)}), bf16[4096,768]{1,0:T(8,128)(2,1)}) %all-gather.2.cloned.1.call-update) | async-done | bytes 6291472 | tf_op jit(solution)/shard_map/all_gather | solution.py:64
  138.7 0.0 copy-done.1
  138.7 0.0 copy-done
  138.7 20.5 %while.14 = (s32[]{:T(128)}, f32[1024]{0:T(1024)S(1)}, s32[128,8]{1,0:T(8,128)}, s32[8,512]{1,0:T(8,128)S(1)}, bf16[8,512,768]{2,1,0:T(8,128)(2,1)}, /*index=5*/...) while((s32[]{:T(128)}, f32[1024]{0:T(1024)S(1)}, ...), condition=%wide.wide.region_6.7_spmd.clone, body=%wide.wide.region_4.6_spmd.clone.sunk | while | flops 808454144 | bytes 2392183 | solution.py:25
  138.8 2.5 %fusion.22 = f32[1024]{0:T(1024)S(1)} fusion(bf16[1024,768]{1,0:T(8,128)(2,1)S(1)} %get-tuple-element.206, s32[1024]{0:T(1024)S(1)} %get-tuple-element.207, s32[512]{0:T(512)S(1)} %bitcast.32, pred[1024]{0:T(1024)(128)(4,1)S(1)} %broadcast_compare_fusion.3, bf16[8,512,768]{2,1,0:T(8,128)(2,1)} %get-tuple-element.205, s32[]{:T(128)S(6)} %copy.10), kind=kOutput, calls=%fused_computation.4.clone.clone.1 | convolution fusion | flops 808451072 | bytes 2370564 | tf_op jit(solution)/shard_map/while/body/eval_jaxpr/dot_general | solution.py:17
  141.3 2.5 %fusion.22 = f32[1024]{0:T(1024)S(1)} fusion(bf16[1024,768]{1,0:T(8,128)(2,1)S(1)} %get-tuple-element.206, s32[1024]{0:T(1024)S(1)} %get-tuple-element.207, s32[512]{0:T(512)S(1)} %bitcast.32, pred[1024]{0:T(1024)(128)(4,1)S(1)} %broadcast_compare_fusion.3, bf16[8,512,768]{2,1,0:T(8,128)(2,1)} %get-tuple-element.205, s32[]{:T(128)S(6)} %copy.10), kind=kOutput, calls=%fused_computation.4.clone.clone.1 | convolution fusion | flops 808451072 | bytes 2370564 | tf_op jit(solution)/shard_map/while/body/eval_jaxpr/dot_general | solution.py:17
  143.9 2.5 %fusion.22 = f32[1024]{0:T(1024)S(1)} fusion(bf16[1024,768]{1,0:T(8,128)(2,1)S(1)} %get-tuple-element.206, s32[1024]{0:T(1024)S(1)} %get-tuple-element.207, s32[512]{0:T(512)S(1)} %bitcast.32, pred[1024]{0:T(1024)(128)(4,1)S(1)} %broadcast_compare_fusion.3, bf16[8,512,768]{2,1,0:T(8,128)(2,1)} %get-tuple-element.205, s32[]{:T(128)S(6)} %copy.10), kind=kOutput, calls=%fused_computation.4.clone.clone.1 | convolution fusion | flops 808451072 | bytes 2370564 | tf_op jit(solution)/shard_map/while/body/eval_jaxpr/dot_general | solution.py:17
  146.4 2.5 %fusion.22 = f32[1024]{0:T(1024)S(1)} fusion(bf16[1024,768]{1,0:T(8,128)(2,1)S(1)} %get-tuple-element.206, s32[1024]{0:T(1024)S(1)} %get-tuple-element.207, s32[512]{0:T(512)S(1)} %bitcast.32, pred[1024]{0:T(1024)(128)(4,1)S(1)} %broadcast_compare_fusion.3, bf16[8,512,768]{2,1,0:T(8,128)(2,1)} %get-tuple-element.205, s32[]{:T(128)S(6)} %copy.10), kind=kOutput, calls=%fused_computation.4.clone.clone.1 | convolution fusion | flops 808451072 | bytes 2370564 | tf_op jit(solution)/shard_map/while/body/eval_jaxpr/dot_general | solution.py:17
  149.0 2.5 %fusion.22 = f32[1024]{0:T(1024)S(1)} fusion(bf16[1024,768]{1,0:T(8,128)(2,1)S(1)} %get-tuple-element.206, s32[1024]{0:T(1024)S(1)} %get-tuple-element.207, s32[512]{0:T(512)S(1)} %bitcast.32, pred[1024]{0:T(1024)(128)(4,1)S(1)} %broadcast_compare_fusion.3, bf16[8,512,768]{2,1,0:T(8,128)(2,1)} %get-tuple-element.205, s32[]{:T(128)S(6)} %copy.10), kind=kOutput, calls=%fused_computation.4.clone.clone.1 | convolution fusion | flops 808451072 | bytes 2370564 | tf_op jit(solution)/shard_map/while/body/eval_jaxpr/dot_general | solution.py:17
  151.6 2.5 %fusion.22 = f32[1024]{0:T(1024)S(1)} fusion(bf16[1024,768]{1,0:T(8,128)(2,1)S(1)} %get-tuple-element.206, s32[1024]{0:T(1024)S(1)} %get-tuple-element.207, s32[512]{0:T(512)S(1)} %bitcast.32, pred[1024]{0:T(1024)(128)(4,1)S(1)} %broadcast_compare_fusion.3, bf16[8,512,768]{2,1,0:T(8,128)(2,1)} %get-tuple-element.205, s32[]{:T(128)S(6)} %copy.10), kind=kOutput, calls=%fused_computation.4.clone.clone.1 | convolution fusion | flops 808451072 | bytes 2370564 | tf_op jit(solution)/shard_map/while/body/eval_jaxpr/dot_general | solution.py:17
  154.1 2.5 %fusion.22 = f32[1024]{0:T(1024)S(1)} fusion(bf16[1024,768]{1,0:T(8,128)(2,1)S(1)} %get-tuple-element.206, s32[1024]{0:T(1024)S(1)} %get-tuple-element.207, s32[512]{0:T(512)S(1)} %bitcast.32, pred[1024]{0:T(1024)(128)(4,1)S(1)} %broadcast_compare_fusion.3, bf16[8,512,768]{2,1,0:T(8,128)(2,1)} %get-tuple-element.205, s32[]{:T(128)S(6)} %copy.10), kind=kOutput, calls=%fused_computation.4.clone.clone.1 | convolution fusion | flops 808451072 | bytes 2370564 | tf_op jit(solution)/shard_map/while/body/eval_jaxpr/dot_general | solution.py:17
  156.7 2.5 %fusion.22 = f32[1024]{0:T(1024)S(1)} fusion(bf16[1024,768]{1,0:T(8,128)(2,1)S(1)} %get-tuple-element.206, s32[1024]{0:T(1024)S(1)} %get-tuple-element.207, s32[512]{0:T(512)S(1)} %bitcast.32, pred[1024]{0:T(1024)(128)(4,1)S(1)} %broadcast_compare_fusion.3, bf16[8,512,768]{2,1,0:T(8,128)(2,1)} %get-tuple-element.205, s32[]{:T(128)S(6)} %copy.10), kind=kOutput, calls=%fused_computation.4.clone.clone.1 | convolution fusion | flops 808451072 | bytes 2370564 | tf_op jit(solution)/shard_map/while/body/eval_jaxpr/dot_general | solution.py:17
  159.2 0.7 all_to_all.21
  159.9 14.3 %all-to-all-start.2 = ((f32[128,1,8]{2,1,0:T(1,128)}), f32[128,1,8]{2,1,0:T(1,128)S(1)}, u32[]{:S(2)}, u32[]{:S(2)}) async-start(f32[128,1,8]{2,1,0:T(1,128)} %bitcast.5), calls=%async_computation.2 | async-start | bytes 131072 | tf_op jit(solution)/shard_map/all_to_all | solution.py:67
  174.3 11.4 %all-to-all-done.2 = f32[128,1,8]{2,1,0:T(1,128)S(1)} async-done(((f32[128,1,8]{2,1,0:T(1,128)}), f32[128,1,8]{2,1,0:T(1,128)S(1)}, u32[]{:S(2)}, u32[]{:S(2)}) %all-to-all-start.2) | async-done | bytes 4128 | tf_op jit(solution)/shard_map/all_to_all | solution.py:67
  185.7 0.5 broadcast.68
  186.2 0.8 reduce.7
  187.0 0.1 reshape.52
  187.1 3.4 %gather_fusion = f32[512]{0:T(512)} fusion(f32[1024]{0:T(1024)S(1)} %reshape.52, s32[1024]{0:T(1024)S(1)} %pad_clamp_fusion), kind=kCustom, calls=%fused_computation | custom fusion | bytes 6144 | tf_op jit(solution)/shard_map/gather | solution.py:70
  (28 shorter events, 0.2 us)
Async XLA Ops:
  6.5 132.2 %all-gather.2.cloned.1.call-start = ((), (), s32[]{:S(2)}) async-start(), calls=%async_computation.3 | async-start | bytes 7864320 | tf_op jit(solution)/shard_map/all_gather | solution.py:64
  72.8 65.9 %copy-start = (bf16[128,8,768]{2,1,0:T(8,128)(2,1)S(1)}, bf16[128,8,768]{2,1,0:T(8,128)(2,1)}, u32[]{:S(2)}) copy-start(bf16[128,8,768]{2,1,0:T(8,128)(2,1)} %all_to_all.26) | copy-start | bytes 4718596
  76.3 18.9 %all-to-all-start = ((s32[128,1,8]{2,1,0:T(1,128)}), s32[128,1,8]{2,1,0:T(1,128)S(1)}, u32[]{:S(2)}, u32[]{:S(2)}) async-start(s32[128,1,8]{2,1,0:T(1,128)} %bitcast), calls=%async_computation | async-start | bytes 131072 | tf_op jit(solution)/shard_map/all_to_all | solution.py:55
  95.3 43.5 %copy-start.1 = (s32[128,1,8]{2,1,0:T(1,128)}, s32[128,1,8]{2,1,0:T(1,128)S(1)}, u32[]{:S(2)}) copy-start(s32[128,1,8]{2,1,0:T(1,128)S(1)} %all-to-all-done) | copy-start | bytes 12292
  159.9 25.8 %all-to-all-start.2 = ((f32[128,1,8]{2,1,0:T(1,128)}), f32[128,1,8]{2,1,0:T(1,128)S(1)}, u32[]{:S(2)}, u32[]{:S(2)}) async-start(f32[128,1,8]{2,1,0:T(1,128)} %bitcast.5), calls=%async_computation.2 | async-start | bytes 131072 | tf_op jit(solution)/shard_map/all_to_all | solution.py:67
Sparse Core Ops, SparseCore 0:
  73.0 65.6 all-gather.1
where the time goes:
time: 198 us; the launch traced here: 197 us
  blocking collectives  69.9 us (35%)
  waiting for transfers between devices  54.3 us (27%)
  starting transfers between devices  21.9 us (11%)
  matrix products  19.9 us (10%)
  between operations  13.5 us (7%)
  local copies, waits for them, and re-layouts  9.03 us (5%)
  other arithmetic  8.48 us (4%)
    all_to_all x1, blocking collectives, shards(): lax.all_to_all(outgoing.reshape(n_shard, capacity, feature_count), 'shard...  59.6 us
    all_gather x1, waiting for transfers between devices, shards(): lax.all_gather(arrived, 'tile', axis=0, tiled=True)  31.5 us
    dot_general x8, matrix products, advance(): lax.dot_general(query_rows, key_part, (((1,), (1,)), ((), ())), preferred...  19.9 us
    all_to_all x1, starting transfers between devices, shards(): lax.all_to_all(row_sums.reshape(n_shard, capacity), 'shard', split_axis=0...  14.3 us
    all_to_all x1, waiting for transfers between devices, shards(): lax.all_to_all(row_sums.reshape(n_shard, capacity), 'shard', split_axis=0...  11.4 us
    all_to_all x1, waiting for transfers between devices, shards(): lax.all_to_all(slot_ids.reshape(n_shard, capacity), 'shard', split_axis=0...  11.4 us
    all_gather x1, blocking collectives, shards(): lax.all_gather(arrived_ids, 'tile', axis=0, tiled=True)  10.4 us
    all_to_all x1, starting transfers between devices, shards(): lax.all_to_all(slot_ids.reshape(n_shard, capacity), 'shard', split_axis=0...  7.53 us
  transfers between devices with their start and end apart: 3, of which 3 were waited for; matrix products, arithmetic and copies ran while one was open for 2% of the time, Pallas kernels for 0%

commit v1 on v0

v1 whole, which is shorter than its diff:
```python
import functools

import jax
import jax.numpy as jnp
from jax import lax
from jax.experimental import pallas as pl
from jax.experimental.pallas import tpu as pltpu
from jax.sharding import PartitionSpec as P

F32 = jnp.float32
BF16 = jnp.bfloat16
I32 = jnp.int32
MESH = pl.DeviceIdType.MESH
CAP = 8
SCALE = 10.0 * 1.4426950408889634


def iota(shape, dim):
    return lax.broadcasted_iota(I32, shape, dim)


def nt_dot(left, right):
    return lax.dot_general(left, right, (((1,), (1,)), ((), ())), preferred_element_type=F32)


def kernel(
    na, nx, home_ref, cluster_ref, emb_ref, out_ref,
    unit, out1, in1, in2, own, sib, acc,
    ids1, ids1_in, ids2, ids2_in, key_ids, sib_ids, query_ids,
    den, den_in, ret, ret_in,
    send1, recv1, send2, recv2, send3, recv3,
    isend1, irecv1, isend2, irecv2, isend3, irecv3,
    dsend1, drecv1, dsend2, drecv2, local,
):
    nb = na
    nk = 2 * nb // nx
    half = nx // 2
    rows, feat = emb_ref.shape
    hf = feat // 2
    chunk = nb * nx * CAP
    wide = nx * CAP
    per_step = nx * nk * CAP
    lanes = 128

    shard = lax.axis_index("shard")
    x = lax.axis_index("tile")
    core = shard % 2
    y = (shard // 2) % nb
    z = shard // (2 * nb)
    a = z + core * (y - z)
    b = y + core * (z - y)

    def dev(a_to, b_to, x_to):
        z_to = a_to + core * (b_to - a_to)
        y_to = b_to + core * (a_to - b_to)
        return ((z_to * nb + y_to) * 2 + core, x_to)

    sibling = (shard + 1 - 2 * core, x)

    def delta(t):
        return ((t + 1) // 2) * (2 * (t % 2) - 1) + na

    def a_dst(t):
        return (a + delta(t)) % na

    def a_src(t):
        return (a - delta(t) + 2 * na) % na

    def b_dst(k):
        c_to = k // (nb // nx)
        return (x - a - half * c_to + 2 * nx + na * nx) % nx + nx * (k % (nb // nx))

    turn = (x - a - b + 2 * na * nx) % nx
    computes = turn % half == 0
    k_self = (turn // half) * (nb // nx) + b // nx

    barrier = pltpu.get_barrier_semaphore()

    def greet_a(i, carry):
        t, xs = i // nx, i % nx

        @pl.when(i != x)
        def _():
            pl.semaphore_signal(barrier, inc=1, device_id=dev(a_dst(t), b, xs), device_id_type=MESH)
        return carry

    lax.fori_loop(0, na * nx, greet_a, 0)

    def greet_b(i, carry):
        @pl.when(i != b)
        def _():
            pl.semaphore_signal(barrier, inc=1, device_id=dev(a, i, x), device_id_type=MESH)
        return carry

    lax.fori_loop(0, nb, greet_b, 0)
    pl.semaphore_signal(barrier, inc=1, device_id=sibling, device_id_type=MESH)

    home = home_ref[...]
    named = iota((2 * na * nb, rows), 0) == home
    before = (iota((rows, rows), 0) < iota((rows, rows), 1)).astype(BF16)
    counts = jnp.dot(named.astype(BF16), before, preferred_element_type=F32)
    pos = jnp.sum(jnp.where(named, counts, 0.0), axis=0, keepdims=True).astype(I32)
    c_own = home % 2
    y_own = (home // 2) % nb
    z_own = home // (2 * nb)
    a_own = z_own + core * (y_own - z_own)
    b_own = y_own + core * (z_own - y_own)
    x_own = (a_own + b_own + half * c_own) % nx
    k_own = c_own * (nb // nx) + b_own // nx
    step = (a_own - a + na) % na
    step = jnp.where(step <= na // 2, jnp.maximum(2 * step - 1, 0), 2 * (na - step))
    message = step * nx + x_own
    lane = k_own * CAP + pos
    slot = message * (nk * CAP) + lane

    marks = (cluster_ref[...] + 1).astype(F32)
    in_message = (iota((na * nx, rows), 0) == message).astype(BF16)
    in_lane = jnp.where(iota((lanes, rows), 0) == lane, marks, 0.0).astype(BF16)
    tags = nt_dot(in_message, in_lane)
    for m in range(na * nx):
        ids1[m] = tags[m : m + 1]

    values = emb_ref[...].astype(F32)
    unit[...] = (
        values * lax.rsqrt(jnp.sum(values * values, axis=1, keepdims=True) + 1e-06)
    ).astype(BF16)

    pl.semaphore_wait(barrier, na * nx - 1 + nb - 1 + 1)

    def ids1_copy(t, xs):
        return pltpu.make_async_remote_copy(
            src_ref=ids1.at[t * nx + xs], dst_ref=ids1_in.at[t * nx + x],
            send_sem=isend1.at[t, xs], recv_sem=irecv1,
            device_id=dev(a_dst(t), b, xs), device_id_type=MESH,
        )

    def out1_copy(t, xs):
        return pltpu.make_async_remote_copy(
            src_ref=out1.at[t, xs], dst_ref=in1.at[t, x],
            send_sem=send1.at[t, xs], recv_sem=recv1.at[t],
            device_id=dev(a_dst(t), b, xs), device_id_type=MESH,
        )

    def ids1_send(i, carry):
        t, xs = i // nx, i % nx

        @pl.when(i != x)
        def _():
            ids1_copy(t, xs).start()

        @pl.when(i == x)
        def _():
            pltpu.make_async_copy(ids1.at[x], ids1_in.at[x], irecv1).start()
        return carry

    lax.fori_loop(0, na * nx, ids1_send, 0)

    def place(t, carry):
        pick = (iota((per_step, rows), 0) + t * per_step == slot).astype(BF16)
        placed = jnp.dot(pick, unit[...], preferred_element_type=F32)
        placed = placed.reshape(nx * nk, CAP, feat)
        placed = jnp.concatenate([placed[:, :, :hf], placed[:, :, hf:]], axis=1).astype(BF16)
        out1[t] = placed.reshape(nx, nk, 2 * CAP, hf)
        for xs in range(nx):
            @pl.when((t > 0) | (xs != x))
            def _():
                out1_copy(t, xs).start()

            @pl.when((t == 0) & (xs == x))
            def _():
                pltpu.make_async_copy(out1.at[0, x], in1.at[0, x], recv1.at[0]).start()
        return carry

    lax.fori_loop(0, na, place, 0)

    pltpu.make_async_copy(ids1, ids1_in, irecv1).wait()
    tags_in = [
        jnp.concatenate([ids1_in[t * nx + xs] for t in range(na)], axis=0) for xs in range(nx)
    ]
    at_lane = iota((na, lanes), 1)

    def shifted(block, source, target):
        kept = jnp.where((at_lane >= source * CAP) & (at_lane < source * CAP + CAP), block, 0.0)
        turns = ((target - source) * CAP) % lanes
        return pltpu.roll(kept, turns, 1) if turns else kept

    for k in range(nk):
        ids2[k] = functools.reduce(jnp.add, [shifted(tags_in[xs], k, xs) for xs in range(nx)])

    def ids2_copy(k):
        return pltpu.make_async_remote_copy(
            src_ref=ids2.at[k], dst_ref=ids2_in.at[b],
            send_sem=isend2.at[k], recv_sem=irecv2,
            device_id=dev(a, b_dst(k), x), device_id_type=MESH,
        )

    def rows2_copy(t, k):
        return pltpu.make_async_remote_copy(
            src_ref=in1.at[t, :, k], dst_ref=in2.at[t, b],
            send_sem=send2.at[t, k], recv_sem=recv2.at[t],
            device_id=dev(a, b_dst(k), x), device_id_type=MESH,
        )

    for k in range(nk):
        @pl.when(b_dst(k) != b)
        def _():
            ids2_copy(k).start()

        @pl.when(b_dst(k) == b)
        def _():
            pltpu.make_async_copy(ids2.at[k], ids2_in.at[b], irecv2).start()

    def sib_ids_copy():
        return pltpu.make_async_remote_copy(
            src_ref=key_ids, dst_ref=sib_ids, send_sem=isend3, recv_sem=irecv3,
            device_id=sibling, device_id_type=MESH,
        )

    def sib_rows_copy(t):
        return pltpu.make_async_remote_copy(
            src_ref=own.at[t], dst_ref=sib.at[t], send_sem=send3.at[t], recv_sem=recv3.at[t],
            device_id=sibling, device_id_type=MESH,
        )

    def spread_ids():
        pltpu.make_async_copy(ids2_in, ids2_in, irecv2).wait()
        same = iota((chunk, lanes), 1) == iota((chunk, lanes), 0) % wide
        for t in range(na):
            block = jnp.concatenate(
                [jnp.broadcast_to(ids2_in[j, t : t + 1, :], (wide, lanes)) for j in range(nb)],
                axis=0,
            )
            block = jnp.where(same, block, 0.0)
            query_ids[t] = jnp.broadcast_to(
                jnp.sum(block, axis=1, keepdims=True), (chunk, lanes)
            )
            key_ids[t] = nt_dot(jnp.ones((8, lanes), BF16), block.astype(BF16))
        sib_ids_copy().start()
        acc[...] = jnp.zeros_like(acc)

    def add_pairs(q, keys, ids, t):
        scores = nt_dot(own[q], keys[t])
        weights = jnp.exp2(scores * SCALE)
        mine = query_ids[q]
        theirs = ids[t, 0:1, :]
        total = acc[q]
        for j in range(0, chunk, lanes):
            total += jnp.where(mine == theirs[:, j : j + lanes], weights[:, j : j + lanes], 0.0)
        acc[q] = total

    def pair_sums(t, carry):
        pltpu.make_async_copy(in2.at[t], in2.at[t], recv2.at[t]).wait()
        block = in2[t].reshape(nb * nx, 2 * CAP, hf).astype(F32)
        block = jnp.concatenate([block[:, :CAP, :], block[:, CAP:, :]], axis=2)
        own[t] = block.reshape(chunk, feat).astype(BF16)
        sib_rows_copy(t).start()

        def own_pairs(i, c):
            fresh = i <= t
            add_pairs(jnp.where(fresh, i, t), own, key_ids, jnp.where(fresh, t, i - t - 1))
            return c

        lax.fori_loop(0, 2 * t + 1, own_pairs, 0)
        sib_rows_copy(t).wait_recv()

        def sib_pairs(i, c):
            fresh = i <= t
            add_pairs(jnp.where(fresh, i, t), sib, sib_ids, jnp.where(fresh, t, i - t - 1))
            return c

        lax.fori_loop(0, 2 * t + 1, sib_pairs, 0)
        return carry

    def forward(t, carry):
        pltpu.make_async_copy(in1.at[t], in1.at[t], recv1.at[t]).wait()
        for k in range(nk):
            @pl.when(b_dst(k) != b)
            def _():
                rows2_copy(t, k).start()

            @pl.when(b_dst(k) == b)
            def _():
                pltpu.make_async_copy(in1.at[t, :, k], in2.at[t, b], recv2.at[t]).start()

        @pl.when(computes & (t == 0))
        def _():
            spread_ids()
            sib_ids_copy().wait_recv()

        @pl.when(computes & (t > 0))
        def _():
            pair_sums(t - 1, 0)
        return carry

    lax.fori_loop(0, na, forward, 0)

    def den1_copy(to):
        return pltpu.make_async_remote_copy(
            src_ref=den.at[to], dst_ref=den_in.at[k_self],
            send_sem=dsend1.at[to], recv_sem=drecv1,
            device_id=dev(a, to, x), device_id_type=MESH,
        )

    @pl.when(computes)
    def _():
        pair_sums(na - 1, 0)
        same = iota((chunk, lanes), 1) == iota((chunk, lanes), 0) % wide
        for t in range(na):
            sums = jnp.sum(acc[t], axis=1, keepdims=True) * (2.0 ** (-SCALE))
            block = jnp.where(same, sums, 0.0).reshape(nb, wide, lanes)
            block = jnp.sum(block, axis=1)
            for j in range(nb):
                den[j, t : t + 1, :] = block[j : j + 1]

        def den1_send(to, carry):
            @pl.when(to != b)
            def _():
                den1_copy(to).start()

            @pl.when(to == b)
            def _():
                pltpu.make_async_copy(den.at[b], den_in.at[k_self], drecv1).start()
            return carry

        lax.fori_loop(0, nb, den1_send, 0)

    pltpu.make_async_copy(den_in, den_in, drecv1).wait()
    for xs in range(nx):
        block = functools.reduce(jnp.add, [shifted(den_in[k], xs, k) for k in range(nk)])
        for t in range(na):
            ret[t * nx + xs] = block[t : t + 1]

    def ret_copy(t, xs):
        return pltpu.make_async_remote_copy(
            src_ref=ret.at[t * nx + xs], dst_ref=ret_in.at[t * nx + x],
            send_sem=dsend2.at[t, xs], recv_sem=drecv2,
            device_id=dev(a_src(t), b, xs), device_id_type=MESH,
        )

    def ret_send(i, carry):
        t, xs = i // nx, i % nx

        @pl.when(i != x)
        def _():
            ret_copy(t, xs).start()

        @pl.when(i == x)
        def _():
            pltpu.make_async_copy(ret.at[x], ret_in.at[x], drecv2).start()
        return carry

    lax.fori_loop(0, na * nx, ret_send, 0)
    pltpu.make_async_copy(ret, ret_in, drecv2).wait()

    table = jnp.concatenate(
        [ret_in[m] for m in range(na * nx)] + [jnp.zeros((lanes - na * nx, lanes), F32)], axis=0
    )
    table = table.T[: nk * CAP]
    chosen = (iota((lanes, rows), 0) == message).astype(BF16)
    high = table.astype(BF16)
    rest = table - high.astype(F32)
    mid = rest.astype(BF16)
    low = (rest - mid.astype(F32)).astype(BF16)
    picked = (
        jnp.dot(low, chosen, preferred_element_type=F32)
        + jnp.dot(mid, chosen, preferred_element_type=F32)
    ) + jnp.dot(high, chosen, preferred_element_type=F32)
    out_ref[...] = jnp.sum(
        jnp.where(iota((nk * CAP, rows), 0) == lane, picked, 0.0), axis=0, keepdims=True
    )

    def drain_a(i, carry):
        t, xs = i // nx, i % nx

        @pl.when(i != x)
        def _():
            ids1_copy(t, xs).wait_send()
            out1_copy(t, xs).wait_send()
            ret_copy(t, xs).wait_send()
        return carry

    lax.fori_loop(0, na * nx, drain_a, 0)
    for k in range(nk):
        @pl.when(b_dst(k) != b)
        def _():
            ids2_copy(k).wait_send()

            def drain_b(t, carry):
                rows2_copy(t, k).wait_send()
                return carry

            lax.fori_loop(0, na, drain_b, 0)

    @pl.when(computes)
    def _():
        sib_ids_copy().wait_send()

        def drain_c(t, carry):
            sib_rows_copy(t).wait_send()

            @pl.when(t != b)
            def _():
                den1_copy(t).wait_send()
            return carry

        lax.fori_loop(0, na, drain_c, 0)


def shards(n_tile, embeddings, cluster, home):
    n_shard = lax.axis_size("shard")
    na = next(n for n in range(1, n_shard + 1) if 2 * n * n == n_shard)
    nx = n_tile
    nk = 2 * na // nx
    rows, feat = embeddings.shape
    chunk = na * nx * CAP
    hf = feat // 2
    messages = na * nx
    vmem = pltpu.VMEM
    dma = pltpu.SemaphoreType.DMA
    out = pl.pallas_call(
        functools.partial(kernel, na, nx),
        out_shape=jax.ShapeDtypeStruct((1, rows), F32),
        in_specs=[pl.BlockSpec(memory_space=pltpu.VMEM)] * 3,
        out_specs=pl.BlockSpec(memory_space=pltpu.VMEM),
        scratch_shapes=[
            vmem((rows, feat), BF16),
            vmem((na, nx, nk, 2 * CAP, hf), BF16),
            vmem((na, nx, nk, 2 * CAP, hf), BF16),
            vmem((na, na, nx, 2 * CAP, hf), BF16),
            vmem((na, chunk, feat), BF16),
            vmem((na, chunk, feat), BF16),
            vmem((na, chunk, 128), F32),
            vmem((messages, 1, 128), F32),
            vmem((messages, 1, 128), F32),
            vmem((nk, na, 128), F32),
            vmem((na, na, 128), F32),
            vmem((na, 8, chunk), F32),
            vmem((na, 8, chunk), F32),
            vmem((na, chunk, 128), F32),
            vmem((na, na, 128), F32),
            vmem((nk, na, 128), F32),
            vmem((messages, 1, 128), F32),
            vmem((messages, 1, 128), F32),
            dma((na, nx)), dma((na,)), dma((na, nk)), dma((na,)), dma((na,)), dma((na,)),
            dma((na, nx)), dma(()), dma((nk,)), dma(()), dma(()), dma(()),
            dma((na,)), dma(()), dma((na, nx)), dma(()), dma(()),
        ],
        compiler_params=pltpu.CompilerParams(
            collective_id=0, has_side_effects=True, vmem_limit_bytes=48 * 2**20
        ),
    )(home.reshape(1, rows), cluster.reshape(1, rows), embeddings)
    return out.reshape(rows)


def solution(mesh):
    return jax.shard_map(
        functools.partial(shards, mesh.shape["tile"]),
        mesh=mesh,
        in_specs=(P(("shard", "tile"), None), P(("shard", "tile")), P(("shard", "tile"))),
        out_specs=P(("shard", "tile")),
        check_vma=False,
    )
```

time: 198 us -> 117 us (0.59)
  Pallas kernels: 0 us -> 114 us
  blocking collectives: 69.9 us -> 0 us
  waiting for transfers between devices: 54.3 us -> 0 us
  starting transfers between devices: 21.9 us -> 0 us
  matrix products: 19.9 us -> 0 us
  between operations: 13.5 us -> 0.01 us
  other arithmetic: 8.48 us -> 0 us
  local copies, waits for them, and re-layouts: 9.03 us -> 3.08 us
    pallas_call x0 -> x1, Pallas kernels: none -> 114 us  [shards(): pl.pallas_call(functools.partial(kernel, na, nx), out_shape=jax.ShapeDtyp...]
    all_to_all x1 -> x0, blocking collectives: 59.6 us -> none  [shards(): lax.all_to_all(outgoing.reshape(n_shard, capacity, feature_count), 'shard...]
    all_gather x1 -> x0, waiting for transfers between devices: 31.5 us -> none  [shards(): lax.all_gather(arrived, 'tile', axis=0, tiled=True)]
    all_to_all x2 -> x0, waiting for transfers between devices: 22.8 us -> none  [the longest x1 11.4 us: shards(): lax.all_to_all(row_sums.reshape(n_shard, capacity), 'shard', split_axis=0...]
    all_to_all x2 -> x0, starting transfers between devices: 21.9 us -> none  [the longest x1 14.3 us: shards(): lax.all_to_all(row_sums.reshape(n_shard, capacity), 'shard', split_axis=0...]
    dot_general x8 -> x0, matrix products: 19.9 us -> none  [advance(): lax.dot_general(query_rows, key_part, (((1,), (1,)), ((), ())), preferred...]
    all_gather x1 -> x0, blocking collectives: 10.4 us -> none  [shards(): lax.all_gather(arrived_ids, 'tile', axis=0, tiled=True)]
    scatter x1 -> x0, other arithmetic: 3.67 us -> none  [shards(): jnp.zeros((n_shard * capacity, feature_count), jnp.bfloat16).at[slot_index]]
  transfers between devices with their start and end apart: 3 -> 0, of which waited for: 3 -> 0; matrix products, arithmetic and copies ran while one was open for 2% -> 0% of each run, Pallas kernels for 0% -> 0%
where the time goes in v1:
time: 117 us
  Pallas kernels  114 us (97%)
  local copies, waits for them, and re-layouts  3.08 us (3%)
    pallas_call x1, Pallas kernels, shards(): pl.pallas_call(functools.partial(kernel, na, nx), out_shape=jax.ShapeDtyp...  114 us
    unnamed x7, local copies, waits for them, and re-layouts  3.08 us

profile of v1, /device:TPU:1, one launch (start us, length us, event | category | flops | bytes accessed | tf_op | source)
XLA Modules:
  0.0 116.8 jit_solution(812763540303842229)
XLA Ops:
  0.0 0.0 copy-start.1
  0.0 0.7 copy-done.1
  0.7 0.0 copy-start
  0.7 1.1 copy-done
  1.8 0.0 copy-start.2
  1.8 0.7 copy-done.2
  2.5 113.7 %shard_map.37 = f32[1,512]{1,0:T(1,128)S(1)} custom-call(s32[1,512]{1,0:T(1,128)S(1)} %bitcast.4, s32[1,512]{1,0:T(1,128)S(1)} %bitcast.5, bf16[512,768]{1,0:T(8,128)(2,1)S(1)} %copy-done), custom_call_target="tpu_custom_call" | custom-call | tf_op jit(solution)/shard_map/pallas_call | solution.py:420
  116.2 0.6 copy.5
Async XLA Ops:
  0.0 0.7 copy-start.1
  0.7 1.1 copy-start
  1.8 0.7 copy-start.2

commit v2 on v1

v2 whole, which is shorter than its diff:
```python
import functools

import jax
import jax.numpy as jnp
from jax import lax
from jax.experimental import pallas as pl
from jax.experimental.pallas import tpu as pltpu
from jax.sharding import PartitionSpec as P

F32 = jnp.float32
BF16 = jnp.bfloat16
I32 = jnp.int32
MESH = pl.DeviceIdType.MESH
CAP = 8
SCALE = 10.0 * 1.4426950408889634


def iota(shape, dim):
    return lax.broadcasted_iota(I32, shape, dim)


def nt_dot(left, right):
    return lax.dot_general(left, right, (((1,), (1,)), ((), ())), preferred_element_type=F32)


def kernel(
    na, nx, home_hbm, cluster_hbm, emb_hbm, out_ref,
    home_ref, cluster_ref, emb_ref, unit, out1, in1, in2, sib_in, kept, acc, col,
    ids1, ids1_in, ids2, ids2_in, ids2_sib, key_ids, row_ids,
    den, den_in, ret, ret_in,
    load, send1, recv1, send2, recv2, send3, recv3,
    isend1, irecv1, isend2, irecv2, isend3, irecv3,
    dsend1, drecv1, dsend2, drecv2,
):
    nb = na
    nk = 2 * nb // nx
    nj = nb // nx
    half = nx // 2
    rows, feat = emb_ref.shape
    hf = feat // 2
    chunk = nb * nx * CAP
    wide = nx * CAP
    per_step = nx * nk * CAP
    lanes = 128
    group = 4

    loads = [
        pltpu.make_async_copy(src, dst, load.at[i])
        for i, (src, dst) in enumerate(
            [(home_hbm, home_ref), (cluster_hbm, cluster_ref), (emb_hbm, emb_ref)]
        )
    ]
    for copy in loads:
        copy.start()

    shard = lax.axis_index("shard")
    x = lax.axis_index("tile")
    core = lax.rem(shard, 2)
    y = lax.rem(lax.div(shard, 2), nb)
    z = lax.div(shard, 2 * nb)
    a = z + core * (y - z)
    b = y + core * (z - y)

    def on(a_to, b_to):
        z_to = a_to + core * (b_to - a_to)
        y_to = b_to + core * (a_to - b_to)
        return (z_to * nb + y_to) * 2 + core

    sibling = (shard + 1 - 2 * core, x)

    def delta(t):
        return ((t + 1) // 2 * (2 * (t % 2) - 1)) % na

    ahead = [on(lax.rem(a + delta(t), na), b) for t in range(na)]
    behind = [on(lax.rem(a + na - delta(t), na), b) for t in range(na)]
    ring = [on(a, i) for i in range(nb)]
    b_to = [lax.rem(x - a - half * (k // nj) + nx + na * nx, nx) + nx * (k % nj) for k in range(nk)]
    owner = [on(a, b_to[k]) for k in range(nk)]
    stays = [b_to[k] == b for k in range(nk)]
    turn = lax.rem(x - a - b + 2 * na * nx, nx)
    computes = lax.rem(turn, half) == 0
    k_self = lax.div(turn, half) * nj + lax.div(b, nx)

    def either(same, local, remote):
        pl.when(same)(local)
        pl.when(jnp.logical_not(same))(remote)

    barrier = pltpu.get_barrier_semaphore()

    def greet(device):
        pl.semaphore_signal(barrier, inc=1, device_id=device, device_id_type=MESH)

    for t in range(na):
        for xs in range(nx):
            if t == 0:
                @pl.when(x != xs)
                def _():
                    greet((ahead[t], xs))
            else:
                greet((ahead[t], xs))
    for i in range(nb):
        @pl.when(b != i)
        def _():
            greet((ring[i], x))
    greet(sibling)

    loads[0].wait()
    home = home_ref[...]
    named = iota((2 * na * nb, rows), 0) == home
    before = (iota((rows, rows), 0) < iota((rows, rows), 1)).astype(BF16)
    counts = jnp.dot(named.astype(BF16), before, preferred_element_type=F32)
    pos = jnp.sum(jnp.where(named, counts, 0.0), axis=0, keepdims=True).astype(I32)
    c_own = home % 2
    y_own = (home // 2) % nb
    z_own = home // (2 * nb)
    a_own = z_own + core * (y_own - z_own)
    b_own = y_own + core * (z_own - y_own)
    x_own = (a_own + b_own + half * c_own) % nx
    k_own = c_own * nj + b_own // nx
    step = (a_own - a + na) % na
    step = jnp.where(step <= na // 2, jnp.maximum(2 * step - 1, 0), 2 * (na - step))
    message = step * nx + x_own
    lane = k_own * CAP + pos
    slot = message * (nk * CAP) + lane

    loads[2].wait()
    values = emb_ref[...].astype(F32)
    unit[...] = (
        values * lax.rsqrt(jnp.sum(values * values, axis=1, keepdims=True) + 1e-06)
    ).astype(BF16)

    loads[1].wait()
    marks = (cluster_ref[...] + 1).astype(F32)
    in_message = (iota((na * nx, rows), 0) == message).astype(BF16)
    in_lane = jnp.where(iota((lanes, rows), 0) == lane, marks, 0.0).astype(BF16)
    tags = nt_dot(in_message, in_lane)
    for m in range(na * nx):
        ids1[m] = tags[m : m + 1]

    pl.semaphore_wait(barrier, na * nx - 1 + nb - 1 + 1)

    def ids1_copy(t, xs):
        return pltpu.make_async_remote_copy(
            src_ref=ids1.at[t * nx + xs], dst_ref=ids1_in.at[t * nx + x],
            send_sem=isend1.at[t, xs], recv_sem=irecv1,
            device_id=(ahead[t], xs), device_id_type=MESH,
        )

    def out1_copy(t, xs):
        return pltpu.make_async_remote_copy(
            src_ref=out1.at[t, xs], dst_ref=in1.at[t, x],
            send_sem=send1.at[t, xs], recv_sem=recv1.at[t],
            device_id=(ahead[t], xs), device_id_type=MESH,
        )

    def place(t):
        pick = (iota((per_step, rows), 0) + t * per_step == slot).astype(BF16)
        placed = jnp.dot(pick, unit[...], preferred_element_type=F32)
        placed = placed.reshape(nx * nk, CAP, feat)
        placed = jnp.concatenate([placed[:, :, :hf], placed[:, :, hf:]], axis=1).astype(BF16)
        out1[t] = placed.reshape(nx, nk, 2 * CAP, hf)
        for xs in range(nx):
            if t > 0:
                out1_copy(t, xs).start()
            else:
                either(
                    x == xs,
                    lambda: pltpu.make_async_copy(out1.at[0, x], in1.at[0, x], recv1.at[0]).start(),
                    lambda: out1_copy(t, xs).start(),
                )

    def ids1_send():
        for t in range(na):
            for xs in range(nx):
                if t > 0:
                    ids1_copy(t, xs).start()
                else:
                    either(
                        x == xs,
                        lambda: pltpu.make_async_copy(ids1.at[x], ids1_in.at[x], irecv1).start(),
                        lambda: ids1_copy(t, xs).start(),
                    )

    for t in range(na):
        if t == min(3, na - 1):
            ids1_send()
        place(t)

    at_lane = iota((na, lanes), 1)

    def shifted(block, source, target):
        mine = jnp.where((at_lane >= source * CAP) & (at_lane < source * CAP + CAP), block, 0.0)
        turns = ((target - source) * CAP) % lanes
        return pltpu.roll(mine, turns, 1) if turns else mine

    def ids2_copy(k):
        return pltpu.make_async_remote_copy(
            src_ref=ids2.at[k], dst_ref=ids2_in.at[b],
            send_sem=isend2.at[k], recv_sem=irecv2,
            device_id=(owner[k], x), device_id_type=MESH,
        )

    def rows2_copy(t, k):
        return pltpu.make_async_remote_copy(
            src_ref=in1.at[t, :, k], dst_ref=in2.at[t, b],
            send_sem=send2.at[t, k], recv_sem=recv2.at[t],
            device_id=(owner[k], x), device_id_type=MESH,
        )

    def forward_ids():
        pltpu.make_async_copy(ids1, ids1_in, irecv1).wait()
        tags_in = [
            jnp.concatenate([ids1_in[t * nx + xs] for t in range(na)], axis=0)
            for xs in range(nx)
        ]
        for k in range(nk):
            ids2[k] = functools.reduce(jnp.add, [shifted(tags_in[xs], k, xs) for xs in range(nx)])
            either(
                stays[k],
                lambda: pltpu.make_async_copy(ids2.at[k], ids2_in.at[b], irecv2).start(),
                lambda: ids2_copy(k).start(),
            )

    for t in range(na):
        pltpu.make_async_copy(in1.at[t], in1.at[t], recv1.at[t]).wait()
        for k in range(nk):
            either(
                stays[k],
                lambda: pltpu.make_async_copy(
                    in1.at[t, :, k], in2.at[t, b], recv2.at[t]
                ).start(),
                lambda: rows2_copy(t, k).start(),
            )
        if t == min(2, na - 1):
            forward_ids()

    for t in range(na):
        for xs in range(nx):
            def sent(t=t, xs=xs):
                ids1_copy(t, xs).wait_send()
                out1_copy(t, xs).wait_send()

            if t > 0:
                sent()
            else:
                pl.when(x != xs)(sent)

    def sib_ids_copy():
        return pltpu.make_async_remote_copy(
            src_ref=ids2_in, dst_ref=ids2_sib, send_sem=isend3, recv_sem=irecv3,
            device_id=sibling, device_id_type=MESH,
        )

    def sib_rows_copy(t):
        return pltpu.make_async_remote_copy(
            src_ref=kept.at[0, t], dst_ref=sib_in.at[t],
            send_sem=send3.at[t], recv_sem=recv3.at[t],
            device_id=sibling, device_id_type=MESH,
        )

    def spread_ids(source, side):
        same = iota((chunk, lanes), 1) == iota((chunk, lanes), 0) % wide

        def spread(t, carry):
            block = jnp.concatenate(
                [
                    jnp.broadcast_to(source[j, pl.ds(t, 1), :], (wide, lanes))
                    for j in range(nb)
                ],
                axis=0,
            )
            block = jnp.where(same, block, 0.0)
            row_ids[side, t] = jnp.broadcast_to(
                jnp.sum(block, axis=1, keepdims=True), (chunk, lanes)
            )
            key_ids[side, t] = nt_dot(jnp.ones((8, lanes), BF16), block.astype(BF16))
            return carry

        lax.fori_loop(0, na, spread, 0)

    def tile(side, g, key_side, t, last, by_row, by_col, sums):
        left = kept[side, pl.ds(g * group, group)].reshape(group * chunk, feat)
        scores = nt_dot(left, kept[key_side, t])
        weights = jnp.exp2(scores * SCALE)
        theirs = key_ids[key_side, t, 0:1, :]
        for i in range(group):
            at = g * group + i
            mine = row_ids[side, at]
            valid = jnp.where(at <= last, theirs, -1.0)
            matched = [
                jnp.where(
                    mine == valid[:, j : j + lanes],
                    weights[i * chunk : (i + 1) * chunk, j : j + lanes],
                    0.0,
                )
                for j in range(0, chunk, lanes)
            ]
            if by_row:
                acc[at] += functools.reduce(jnp.add, matched)
            if by_col:
                parts = [jnp.sum(m.reshape(chunk // 8, 8, lanes), axis=0) for m in matched]
                part = jnp.concatenate(parts, axis=1)
                if by_row:
                    part = jnp.where(at < t, part, 0.0)
                sums += part
        return sums

    def pair_sums(t, carry):
        pltpu.make_async_copy(in2.at[t], in2.at[t], recv2.at[t]).wait()
        block = in2[t].reshape(nb * nx, 2 * CAP, hf).astype(F32)
        block = jnp.concatenate([block[:, :CAP, :], block[:, CAP:, :]], axis=2)
        kept[0, t] = block.reshape(chunk, feat).astype(BF16)
        sib_rows_copy(t).start()
        groups = lax.div(t + group, group)
        sums = lax.fori_loop(
            0, groups, lambda g, c: tile(0, g, 0, t, t, True, True, c),
            jnp.zeros((8, chunk), F32),
        )

        @pl.when(t == 0)
        def _():
            sib_ids_copy().wait_recv()
            spread_ids(ids2_sib, 1)

        sib_rows_copy(t).wait_recv()
        kept[1, t] = sib_in[t]
        sums = lax.fori_loop(
            0, groups, lambda g, c: tile(1, g, 0, t, t, False, True, c), sums
        )
        col[pl.ds(t, 1), :] = jnp.sum(sums, axis=0, keepdims=True)
        lax.fori_loop(
            0, lax.div(t + group - 1, group),
            lambda g, c: tile(0, g, 1, t, t - 1, True, False, c), 0,
        )
        return carry

    def den1_copy(to):
        return pltpu.make_async_remote_copy(
            src_ref=den.at[to], dst_ref=den_in.at[k_self],
            send_sem=dsend1.at[to], recv_sem=drecv1,
            device_id=(ring[to], x), device_id_type=MESH,
        )

    @pl.when(computes)
    def _():
        pltpu.make_async_copy(ids2_in, ids2_in, irecv2).wait()
        sib_ids_copy().start()
        spread_ids(ids2_in, 0)
        acc[...] = jnp.zeros_like(acc)
        lax.fori_loop(0, na, pair_sums, 0)

        same = iota((chunk, lanes), 1) == iota((chunk, lanes), 0) % wide
        for t in range(na):
            sums = jnp.sum(acc[t], axis=1, keepdims=True)
            block = jnp.where(same, sums, 0.0).reshape(nb, wide, lanes)
            block = jnp.sum(block, axis=1)
            for j in range(nb):
                den[j, t : t + 1, :] = block[j : j + 1]
        by_col = col[...]
        per = lanes // wide
        for j in range(nb):
            part = by_col[:, j // per * lanes : (j // per + 1) * lanes]
            turns = (-(j % per) * wide) % lanes
            part = pltpu.roll(part, turns, 1) if turns else part
            part = jnp.where(at_lane < wide, part, 0.0)
            den[j] = (den[j] + part) * (2.0 ** (-SCALE))
            either(
                b == j,
                lambda: pltpu.make_async_copy(den.at[j], den_in.at[k_self], drecv1).start(),
                lambda: den1_copy(j).start(),
            )

    for k in range(nk):
        @pl.when(jnp.logical_not(stays[k]))
        def _():
            ids2_copy(k).wait_send()
            for t in range(na):
                rows2_copy(t, k).wait_send()

    pltpu.make_async_copy(den_in, den_in, drecv1).wait()

    def ret_copy(t, xs):
        return pltpu.make_async_remote_copy(
            src_ref=ret.at[t * nx + xs], dst_ref=ret_in.at[t * nx + x],
            send_sem=dsend2.at[t, xs], recv_sem=drecv2,
            device_id=(behind[t], xs), device_id_type=MESH,
        )

    for xs in range(nx):
        block = functools.reduce(jnp.add, [shifted(den_in[k], xs, k) for k in range(nk)])
        for t in range(na):
            ret[t * nx + xs] = block[t : t + 1]
            if t > 0:
                ret_copy(t, xs).start()
            else:
                either(
                    x == xs,
                    lambda: pltpu.make_async_copy(ret.at[x], ret_in.at[x], drecv2).start(),
                    lambda: ret_copy(t, xs).start(),
                )

    @pl.when(computes)
    def _():
        sib_ids_copy().wait_send()
        for t in range(na):
            sib_rows_copy(t).wait_send()

            @pl.when(b != t)
            def _():
                den1_copy(t).wait_send()

    chosen = (iota((lanes, rows), 0) == message).astype(BF16)
    pltpu.make_async_copy(ret, ret_in, drecv2).wait()

    table = jnp.concatenate(
        [ret_in[m] for m in range(na * nx)] + [jnp.zeros((lanes - na * nx, lanes), F32)], axis=0
    )
    table = table.T[: nk * CAP]
    high = table.astype(BF16)
    rest = table - high.astype(F32)
    mid = rest.astype(BF16)
    low = (rest - mid.astype(F32)).astype(BF16)
    picked = (
        jnp.dot(low, chosen, preferred_element_type=F32)
        + jnp.dot(mid, chosen, preferred_element_type=F32)
    ) + jnp.dot(high, chosen, preferred_element_type=F32)
    out_ref[...] = jnp.sum(
        jnp.where(iota((nk * CAP, rows), 0) == lane, picked, 0.0), axis=0, keepdims=True
    )

    for t in range(na):
        for xs in range(nx):
            if t > 0:
                ret_copy(t, xs).wait_send()
            else:
                @pl.when(x != xs)
                def _():
                    ret_copy(t, xs).wait_send()


def shards(n_tile, embeddings, cluster, home):
    n_shard = lax.axis_size("shard")
    na = next(n for n in range(1, n_shard + 1) if 2 * n * n == n_shard)
    nx = n_tile
    nk = 2 * na // nx
    rows, feat = embeddings.shape
    chunk = na * nx * CAP
    hf = feat // 2
    messages = na * nx
    vmem = pltpu.VMEM
    dma = pltpu.SemaphoreType.DMA
    out = pl.pallas_call(
        functools.partial(kernel, na, nx),
        out_shape=jax.ShapeDtypeStruct((1, rows), F32),
        in_specs=[pl.BlockSpec(memory_space=pl.ANY)] * 3,
        out_specs=pl.BlockSpec(memory_space=pltpu.VMEM),
        scratch_shapes=[
            vmem((1, rows), I32),
            vmem((1, rows), I32),
            vmem((rows, feat), BF16),
            vmem((rows, feat), BF16),
            vmem((na, nx, nk, 2 * CAP, hf), BF16),
            vmem((na, nx, nk, 2 * CAP, hf), BF16),
            vmem((na, na, nx, 2 * CAP, hf), BF16),
            vmem((na, chunk, feat), BF16),
            vmem((2, na, chunk, feat), BF16),
            vmem((na, chunk, 128), F32),
            vmem((na, chunk), F32),
            vmem((messages, 1, 128), F32),
            vmem((messages, 1, 128), F32),
            vmem((nk, na, 128), F32),
            vmem((na, na, 128), F32),
            vmem((na, na, 128), F32),
            vmem((2, na, 8, chunk), F32),
            vmem((2, na, chunk, 128), F32),
            vmem((na, na, 128), F32),
            vmem((nk, na, 128), F32),
            vmem((messages, 1, 128), F32),
            vmem((messages, 1, 128), F32),
            dma((3,)),
            dma((na, nx)), dma((na,)), dma((na, nk)), dma((na,)), dma((na,)), dma((na,)),
            dma((na, nx)), dma(()), dma((nk,)), dma(()), dma(()), dma(()),
            dma((na,)), dma(()), dma((na, nx)), dma(()),
        ],
        compiler_params=pltpu.CompilerParams(
            collective_id=0, has_side_effects=True, vmem_limit_bytes=48 * 2**20
        ),
    )(home.reshape(1, rows), cluster.reshape(1, rows), embeddings)
    return out.reshape(rows)


def solution(mesh):
    return jax.shard_map(
        functools.partial(shards, mesh.shape["tile"]),
        mesh=mesh,
        in_specs=(P(("shard", "tile"), None), P(("shard", "tile")), P(("shard", "tile"))),
        out_specs=P(("shard", "tile")),
        check_vma=False,
    )
```

time: 117 us -> 104 us (0.89)
  Pallas kernels: 114 us -> 101 us
    pallas_call x1, Pallas kernels: 114 us -> 101 us  [shards(): pl.pallas_call(functools.partial(kernel, na, nx), out_shape=jax.ShapeDtyp...]
where the time goes in v2:
time: 104 us
  Pallas kernels  101 us (97%)
  local copies, waits for them, and re-layouts  3.08 us (3%)
    pallas_call x1, Pallas kernels, shards(): pl.pallas_call(functools.partial(kernel, na, nx), out_shape=jax.ShapeDtyp...  101 us
    unnamed x7, local copies, waits for them, and re-layouts  3.08 us

profile of v2, /device:TPU:1, one launch (start us, length us, event | category | flops | bytes accessed | tf_op | source)
XLA Modules:
  0.0 104.1 jit_solution(11021353608858456551)
XLA Ops:
  0.0 0.0 copy-start.1
  0.0 0.7 copy-done.1
  0.7 0.0 copy-start
  0.7 1.1 %copy-done = bf16[512,768]{1,0:T(8,128)(2,1)S(1)} copy-done((bf16[512,768]{1,0:T(8,128)(2,1)S(1)}, bf16[512,768]{1,0:T(8,128)(2,1)}, u32[]{:S(2)}) %copy-start) | copy-done | bytes 786456
  1.8 0.0 copy-start.2
  1.8 0.7 copy-done.2
  2.5 101.0 %shard_map.37 = f32[1,512]{1,0:T(1,128)S(1)} custom-call(s32[1,512]{1,0:T(1,128)S(1)} %bitcast.4, s32[1,512]{1,0:T(1,128)S(1)} %bitcast.5, bf16[512,768]{1,0:T(8,128)(2,1)S(1)} %copy-done), custom_call_target="tpu_custom_call" | custom-call | tf_op jit(solution)/shard_map/pallas_call | solution.py:452
  103.5 0.6 copy.5
Async XLA Ops:
  0.0 0.7 copy-start.1
  0.7 1.1 %copy-start = (bf16[512,768]{1,0:T(8,128)(2,1)S(1)}, bf16[512,768]{1,0:T(8,128)(2,1)}, u32[]{:S(2)}) copy-start(bf16[512,768]{1,0:T(8,128)(2,1)} %emb_hbm.1) | copy-start | bytes 2359300
  1.8 0.7 copy-start.2

commit v3 on v2

v3 whole, which is shorter than its diff:
```python
import functools

import jax
import jax.numpy as jnp
from jax import lax
from jax.experimental import pallas as pl
from jax.experimental.pallas import tpu as pltpu
from jax.sharding import PartitionSpec as P

F32 = jnp.float32
BF16 = jnp.bfloat16
I32 = jnp.int32
MESH = pl.DeviceIdType.MESH
CAP = 8
SCALE = 10.0 * 1.4426950408889634


def iota(shape, dim):
    return lax.broadcasted_iota(I32, shape, dim)


def nt_dot(left, right):
    return lax.dot_general(left, right, (((1,), (1,)), ((), ())), preferred_element_type=F32)


def kernel(
    na, nx, home_hbm, cluster_hbm, emb_hbm, out_ref,
    home_ref, cluster_ref, emb_ref, unit, out1, in1, in2, sib_in, kept, acc, col,
    ids1, ids1_in, ids2, ids2_in, ids3_in, ids_sib, key_ids, row_ids,
    den, den_in, ret, ret_in,
    load, send1, recv1, send2, recv2, send3, recv3,
    isend1, irecv1, isend2, irecv2, isend3, irecv3, isend4, irecv4,
    dsend1, drecv1, dsend2, drecv2,
):
    nb = na
    nk = 2 * nb // nx
    nj = nb // nx
    half = nx // 2
    rows, feat = emb_ref.shape
    hf = feat // 2
    ns = na // 2
    nq = 2 * nx
    chunk = nb * ns * CAP
    wide = ns * CAP
    lanes = 128
    group = 4

    loads = [
        pltpu.make_async_copy(src, dst, load.at[i])
        for i, (src, dst) in enumerate(
            [(home_hbm, home_ref), (cluster_hbm, cluster_ref), (emb_hbm, emb_ref)]
        )
    ]
    for copy in loads:
        copy.start()

    shard = lax.axis_index("shard")
    x = lax.axis_index("tile")
    core = lax.rem(shard, 2)
    y = lax.rem(lax.div(shard, 2), nb)
    z = lax.div(shard, 2 * nb)
    a = z + core * (y - z)
    b = y + core * (z - y)

    def on(a_to, b_to):
        z_to = a_to + core * (b_to - a_to)
        y_to = b_to + core * (a_to - b_to)
        return (z_to * nb + y_to) * 2 + core

    sibling = (shard + 1 - 2 * core, x)

    def delta(t):
        return ((t + 1) // 2 * (2 * (t % 2) - 1)) % na

    ahead = [on(lax.rem(a + delta(t), na), b) for t in range(na)]
    behind = [on(lax.rem(a + na - delta(t), na), b) for t in range(na)]
    ring = [on(a, i) for i in range(nb)]
    b_to = [lax.rem(x - a - half * (k // nj) + nx + na * nx, nx) + nx * (k % nj) for k in range(nk)]
    owner = [on(a, b_to[k]) for k in range(nk)]
    stays = [b_to[k] == b for k in range(nk)]
    turn = lax.rem(x - a - b + 2 * na * nx, nx)
    computes = lax.rem(turn, half) == 0
    k_self = lax.div(turn, half) * nj + lax.div(b, nx)
    k_sib = lax.div(turn, half) * nj + lax.div(a, nx)

    def either(same, local, remote):
        pl.when(same)(local)
        pl.when(jnp.logical_not(same))(remote)

    def right(j):
        return lax.rem(x + j, nx)

    def left(j):
        return lax.rem(x + nx - j, nx)

    barrier = pltpu.get_barrier_semaphore()

    def greet(device):
        pl.semaphore_signal(barrier, inc=1, device_id=device, device_id_type=MESH)

    for j in range(nx):
        for t in range(na):
            if j + t > 0:
                greet((ahead[t], right(j)))
    for i in range(nb):
        @pl.when(b != i)
        def _():
            greet((ring[i], x))
    greet(sibling)

    loads[0].wait()
    home = home_ref[...]
    named = iota((2 * na * nb, rows), 0) == home
    before = (iota((rows, rows), 0) < iota((rows, rows), 1)).astype(BF16)
    counts = jnp.dot(named.astype(BF16), before, preferred_element_type=F32)
    pos = jnp.sum(jnp.where(named, counts, 0.0), axis=0, keepdims=True).astype(I32)
    c_own = home % 2
    y_own = (home // 2) % nb
    z_own = home // (2 * nb)
    a_own = z_own + core * (y_own - z_own)
    b_own = y_own + core * (z_own - y_own)
    x_own = (a_own + b_own + half * c_own) % nx
    k_own = c_own * nj + b_own // nx
    step = (a_own - a + na) % na
    step = jnp.where(step <= na // 2, jnp.maximum(2 * step - 1, 0), 2 * (na - step))
    offset = (x_own - x + nx) % nx
    message = offset * na + step
    lane = k_own * CAP + pos
    slot = message * (nk * CAP) + lane

    loads[2].wait()
    values = emb_ref[...].astype(F32)
    unit[...] = (
        values * lax.rsqrt(jnp.sum(values * values, axis=1, keepdims=True) + 1e-06)
    ).astype(BF16)

    loads[1].wait()
    marks = (cluster_ref[...] + 1).astype(F32)
    in_step = (iota((na, rows), 0) == step).astype(BF16)
    in_lane = jnp.where(iota((lanes, rows), 0) == offset * (nk * CAP) + lane, marks, 0.0)
    tags = nt_dot(in_step, in_lane.astype(BF16))
    for t in range(na):
        ids1[t] = tags[t : t + 1]

    pl.semaphore_wait(barrier, na * nx - 1 + nb - 1 + 1)

    def ids1_copy(t):
        return pltpu.make_async_remote_copy(
            src_ref=ids1.at[t], dst_ref=ids1_in.at[t],
            send_sem=isend1.at[t], recv_sem=irecv1,
            device_id=(ahead[t], x), device_id_type=MESH,
        )

    def ids2_copy(i):
        return pltpu.make_async_remote_copy(
            src_ref=ids2, dst_ref=ids2_in.at[b],
            send_sem=isend2.at[i], recv_sem=irecv2,
            device_id=(ring[i], x), device_id_type=MESH,
        )

    def ids3_copy(j):
        return pltpu.make_async_remote_copy(
            src_ref=ids2_in, dst_ref=ids3_in.at[j],
            send_sem=isend3.at[j], recv_sem=irecv3,
            device_id=(shard, right(j)), device_id_type=MESH,
        )

    def out1_copy(j, t):
        q, sub = j * 2 + t // ns, t % ns
        return pltpu.make_async_remote_copy(
            src_ref=out1.at[q, sub], dst_ref=in1.at[q, sub],
            send_sem=send1.at[j, t], recv_sem=recv1.at[j],
            device_id=(ahead[t], right(j)), device_id_type=MESH,
        )

    def place(j, h):
        q = j * 2 + h
        size = ns * nk * CAP
        pick = (iota((size, rows), 0) + q * size == slot).astype(BF16)
        placed = jnp.dot(pick, unit[...], preferred_element_type=F32)
        placed = placed.reshape(ns * nk, CAP, feat)
        placed = jnp.concatenate([placed[:, :, :hf], placed[:, :, hf:]], axis=1).astype(BF16)
        out1[q] = placed.reshape(ns, nk, 2 * CAP, hf)

    def send_stage(j, first):
        for h in range(2):
            place(j, h)
            for t in range(h * ns, (h + 1) * ns):
                if first and t == 0:
                    pltpu.make_async_copy(out1.at[0, 0], in1.at[0, 0], recv1.at[0]).start()
                else:
                    out1_copy(j, t).start()

    def sent_stage(j):
        for t in range(na):
            if t > 0:
                out1_copy(j, t).wait_send()
            else:
                @pl.when(j > 0)
                def _():
                    out1_copy(j, t).wait_send()

    def rows2_copy(q, k):
        return pltpu.make_async_remote_copy(
            src_ref=in1.at[q, :, k], dst_ref=in2.at[q, b],
            send_sem=send2.at[q, k], recv_sem=recv2.at[q],
            device_id=(owner[k], x), device_id_type=MESH,
        )

    def forward_stage(j):
        for h in range(2):
            q = j * 2 + h
            for k in range(nk):
                either(
                    stays[k],
                    lambda: pltpu.make_async_copy(
                        in1.at[q, :, k], in2.at[q, b], recv2.at[q]
                    ).start(),
                    lambda: rows2_copy(q, k).start(),
                )

    def forwarded_stage(j):
        for k in range(nk):
            @pl.when(jnp.logical_not(stays[k]))
            def _():
                for h in range(2):
                    rows2_copy(j * 2 + h, k).wait_send()

    def sib_ids_copy():
        return pltpu.make_async_remote_copy(
            src_ref=ids3_in, dst_ref=ids_sib, send_sem=isend4, recv_sem=irecv4,
            device_id=sibling, device_id_type=MESH,
        )

    def sib_rows_copy(t):
        return pltpu.make_async_remote_copy(
            src_ref=kept.at[0, t], dst_ref=sib_in.at[t],
            send_sem=send3.at[t], recv_sem=recv3.at[t],
            device_id=sibling, device_id_type=MESH,
        )

    def spread_ids(source, side, k):
        def spread(q, carry):
            j, h = lax.div(q, 2), lax.rem(q, 2)
            block = jnp.concatenate(
                [source[j, i, pl.ds(h * ns, ns), :] for i in range(nb)], axis=0
            )
            block = jnp.broadcast_to(block[:, None, :], (nb * ns, CAP, lanes))
            here = iota((nb * ns, CAP, lanes), 1) + (j * nk + k) * CAP
            block = jnp.where(iota((nb * ns, CAP, lanes), 2) == here, block, 0.0)
            block = block.reshape(chunk, lanes)
            row_ids[side, q] = jnp.broadcast_to(
                jnp.sum(block, axis=1, keepdims=True), (chunk, lanes)
            )
            key_ids[side, q] = nt_dot(jnp.ones((8, lanes), BF16), block.astype(BF16))
            return carry

        lax.fori_loop(0, nq, spread, 0)

    def tile(side, g, key_side, t, last, by_row, by_col, sums):
        left = kept[side, pl.ds(g * group, group)].reshape(group * chunk, feat)
        scores = nt_dot(left, kept[key_side, t])
        weights = jnp.exp2(scores * SCALE)
        theirs = key_ids[key_side, t, 0:1, :]
        for i in range(group):
            at = g * group + i
            mine = row_ids[side, at]
            valid = jnp.where(at <= last, theirs, -1.0)
            matched = [
                jnp.where(
                    mine == valid[:, j : j + lanes],
                    weights[i * chunk : (i + 1) * chunk, j : j + lanes],
                    0.0,
                )
                for j in range(0, chunk, lanes)
            ]
            if by_row:
                acc[at] += functools.reduce(jnp.add, matched)
            if by_col:
                parts = [jnp.sum(m.reshape(chunk // 8, 8, lanes), axis=0) for m in matched]
                part = jnp.concatenate(parts, axis=1)
                if by_row:
                    part = jnp.where(at < t, part, 0.0)
                sums += part
        return sums

    def take(t, carry):
        pltpu.make_async_copy(in2.at[t], in2.at[t], recv2.at[t]).wait()
        block = in2[t].reshape(nb * ns, 2 * CAP, hf).astype(F32)
        block = jnp.concatenate([block[:, :CAP, :], block[:, CAP:, :]], axis=2)
        kept[0, t] = block.reshape(chunk, feat).astype(BF16)
        sib_rows_copy(t).start()
        return carry

    def pair_sums(t, carry):
        groups = lax.div(t + group, group)
        sums = lax.fori_loop(
            0, groups, lambda g, c: tile(0, g, 0, t, t, True, True, c),
            jnp.zeros((8, chunk), F32),
        )
        sib_rows_copy(t).wait_recv()
        kept[1, t] = sib_in[t]
        sums = lax.fori_loop(
            0, groups, lambda g, c: tile(1, g, 0, t, t, False, True, c), sums
        )
        col[pl.ds(t, 1), :] = jnp.sum(sums, axis=0, keepdims=True)
        lax.fori_loop(
            0, lax.div(t + group - 1, group),
            lambda g, c: tile(0, g, 1, t, t - 1, True, False, c), 0,
        )
        return carry

    pltpu.make_async_copy(ids1.at[0], ids1_in.at[0], irecv1).start()
    for t in range(1, na):
        ids1_copy(t).start()
    send_stage(0, True)
    pltpu.make_async_copy(ids1, ids1_in, irecv1).wait()
    ids2[...] = jnp.concatenate([ids1_in[t] for t in range(na)], axis=0)
    for i in range(nb):
        either(
            b == i,
            lambda: pltpu.make_async_copy(ids2, ids2_in.at[b], irecv2).start(),
            lambda: ids2_copy(i).start(),
        )
    send_stage(1, False)
    pltpu.make_async_copy(ids2_in, ids2_in, irecv2).wait()
    pltpu.make_async_copy(ids2_in, ids3_in.at[0], irecv3).start()
    for j in range(1, nx):
        ids3_copy(j).start()

    def stage(j, carry):
        @pl.when(j < nx)
        def _():
            here = in1.at[pl.ds(2 * j, 2)]
            pltpu.make_async_copy(here, here, recv1.at[j]).wait()

            @pl.when(j >= 2)
            def _():
                forwarded_stage(j - 2)

            forward_stage(j)

            @pl.when(j < nx - 2)
            def _():
                sent_stage(j)
                send_stage(j + 2, False)

        @pl.when(computes & (j == 0))
        def _():
            pltpu.make_async_copy(ids3_in, ids3_in, irecv3).wait()
            sib_ids_copy().start()
            spread_ids(ids3_in, 0, k_self)
            acc[...] = jnp.zeros_like(acc)

        @pl.when(computes & (j == 1))
        def _():
            sib_ids_copy().wait_recv()
            spread_ids(ids_sib, 1, k_sib)

        @pl.when(computes & (j > 0))
        def _():
            lax.fori_loop(2 * j - 2, 2 * j, take, 0)
            lax.fori_loop(2 * j - 2, 2 * j, pair_sums, 0)
        return carry

    lax.fori_loop(0, nx + 1, stage, 0)

    def den1_copy(to):
        return pltpu.make_async_remote_copy(
            src_ref=den.at[to], dst_ref=den_in.at[k_self],
            send_sem=dsend1.at[to], recv_sem=drecv1,
            device_id=(ring[to], x), device_id_type=MESH,
        )

    @pl.when(computes)
    def _():
        same = iota((chunk, lanes), 1) == iota((chunk, lanes), 0) % wide
        for t in range(nq):
            sums = jnp.sum(acc[t], axis=1, keepdims=True)
            block = jnp.where(same, sums, 0.0).reshape(nb, wide, lanes)
            block = jnp.sum(block, axis=1)
            for j in range(nb):
                den[j, t : t + 1, :] = block[j : j + 1]
        by_col = col[...]
        per = lanes // wide
        for j in range(nb):
            part = by_col[:, j // per * lanes : (j // per + 1) * lanes]
            turns = (-(j % per) * wide) % lanes
            part = pltpu.roll(part, turns, 1) if turns else part
            part = jnp.where(iota((nq, lanes), 1) < wide, part, 0.0)
            den[j] = (den[j] + part) * (2.0 ** (-SCALE))
            either(
                b == j,
                lambda: pltpu.make_async_copy(den.at[j], den_in.at[k_self], drecv1).start(),
                lambda: den1_copy(j).start(),
            )

    @pl.when(jnp.logical_not(computes))
    def _():
        pltpu.make_async_copy(ids3_in, ids3_in, irecv3).wait()

    for j in range(nx - 2, nx):
        sent_stage(j)
        forwarded_stage(j)
    for i in range(1, na):
        ids1_copy(i).wait_send()
    for i in range(nb):
        @pl.when(b != i)
        def _():
            ids2_copy(i).wait_send()
    for j in range(1, nx):
        ids3_copy(j).wait_send()

    at_lane = iota((nq, lanes), 1)

    def shifted(block, source, target):
        mine = jnp.where((at_lane >= source * CAP) & (at_lane < source * CAP + CAP), block, 0.0)
        turns = ((target - source) * CAP) % lanes
        return pltpu.roll(mine, turns, 1) if turns else mine

    pltpu.make_async_copy(den_in, den_in, drecv1).wait()

    def ret_copy(q, sub):
        return pltpu.make_async_remote_copy(
            src_ref=ret.at[q * ns + sub], dst_ref=ret_in.at[q * ns + sub],
            send_sem=dsend2.at[q, sub], recv_sem=drecv2,
            device_id=(behind[q % 2 * ns + sub], left(q // 2)), device_id_type=MESH,
        )

    for sub in range(ns):
        block = functools.reduce(jnp.add, [shifted(den_in[k], sub, k) for k in range(nk)])
        for q in range(nq):
            ret[q * ns + sub] = block[q : q + 1]
            if q + sub > 0:
                ret_copy(q, sub).start()
            else:
                pltpu.make_async_copy(ret.at[0], ret_in.at[0], drecv2).start()

    @pl.when(computes)
    def _():
        sib_ids_copy().wait_send()
        for q in range(nq):
            sib_rows_copy(q).wait_send()
        for i in range(nb):
            @pl.when(b != i)
            def _():
                den1_copy(i).wait_send()

    chosen = (iota((lanes, rows), 0) == message).astype(BF16)
    pltpu.make_async_copy(ret, ret_in, drecv2).wait()

    table = jnp.concatenate(
        [ret_in[m] for m in range(na * nx)] + [jnp.zeros((lanes - na * nx, lanes), F32)], axis=0
    )
    table = table.T[: nk * CAP]
    high = table.astype(BF16)
    rest = table - high.astype(F32)
    mid = rest.astype(BF16)
    low = (rest - mid.astype(F32)).astype(BF16)
    picked = (
        jnp.dot(low, chosen, preferred_element_type=F32)
        + jnp.dot(mid, chosen, preferred_element_type=F32)
    ) + jnp.dot(high, chosen, preferred_element_type=F32)
    out_ref[...] = jnp.sum(
        jnp.where(iota((nk * CAP, rows), 0) == lane, picked, 0.0), axis=0, keepdims=True
    )

    for q in range(nq):
        for sub in range(ns):
            if q + sub > 0:
                ret_copy(q, sub).wait_send()


def shards(n_tile, embeddings, cluster, home):
    n_shard = lax.axis_size("shard")
    na = next(n for n in range(1, n_shard + 1) if 2 * n * n == n_shard)
    nx = n_tile
    nk = 2 * na // nx
    rows, feat = embeddings.shape
    ns = na // 2
    nq = 2 * nx
    chunk = na * ns * CAP
    hf = feat // 2
    messages = na * nx
    vmem = pltpu.VMEM
    dma = pltpu.SemaphoreType.DMA
    out = pl.pallas_call(
        functools.partial(kernel, na, nx),
        out_shape=jax.ShapeDtypeStruct((1, rows), F32),
        in_specs=[pl.BlockSpec(memory_space=pl.ANY)] * 3,
        out_specs=pl.BlockSpec(memory_space=pltpu.VMEM),
        scratch_shapes=[
            vmem((1, rows), I32),
            vmem((1, rows), I32),
            vmem((rows, feat), BF16),
            vmem((rows, feat), BF16),
            vmem((nq, ns, nk, 2 * CAP, hf), BF16),
            vmem((nq, ns, nk, 2 * CAP, hf), BF16),
            vmem((nq, na, ns, 2 * CAP, hf), BF16),
            vmem((nq, chunk, feat), BF16),
            vmem((2, nq, chunk, feat), BF16),
            vmem((nq, chunk, 128), F32),
            vmem((nq, chunk), F32),
            vmem((na, 1, 128), F32),
            vmem((na, 1, 128), F32),
            vmem((na, 128), F32),
            vmem((na, na, 128), F32),
            vmem((nx, na, na, 128), F32),
            vmem((nx, na, na, 128), F32),
            vmem((2, nq, 8, chunk), F32),
            vmem((2, nq, chunk, 128), F32),
            vmem((na, nq, 128), F32),
            vmem((nk, nq, 128), F32),
            vmem((messages, 1, 128), F32),
            vmem((messages, 1, 128), F32),
            dma((3,)),
            dma((nx, na)), dma((nx,)), dma((nq, nk)), dma((nq,)), dma((nq,)), dma((nq,)),
            dma((na,)), dma(()), dma((na,)), dma(()), dma((nx,)), dma(()), dma(()), dma(()),
            dma((na,)), dma(()), dma((nq, ns)), dma(()),
        ],
        compiler_params=pltpu.CompilerParams(
            collective_id=0, has_side_effects=True, vmem_limit_bytes=48 * 2**20
        ),
    )(home.reshape(1, rows), cluster.reshape(1, rows), embeddings)
    return out.reshape(rows)


def solution(mesh):
    return jax.shard_map(
        functools.partial(shards, mesh.shape["tile"]),
        mesh=mesh,
        in_specs=(P(("shard", "tile"), None), P(("shard", "tile")), P(("shard", "tile"))),
        out_specs=P(("shard", "tile")),
        check_vma=False,
    )
```

time: 104 us -> 89 us (0.86)
  Pallas kernels: 101 us -> 85.1 us
    pallas_call x1, Pallas kernels: 101 us -> 85.1 us  [shards(): pl.pallas_call(functools.partial(kernel, na, nx), out_shape=jax.ShapeDtyp...]
where the time goes in v3:
time: 89 us; the launch traced here: 88.2 us
  Pallas kernels  85.1 us (96%)
  local copies, waits for them, and re-layouts  3.08 us (3%)
    pallas_call x1, Pallas kernels, shards(): pl.pallas_call(functools.partial(kernel, na, nx), out_shape=jax.ShapeDtyp...  85.1 us
    unnamed x7, local copies, waits for them, and re-layouts  3.08 us

profile of v3, /device:TPU:1, one launch (start us, length us, event | category | flops | bytes accessed | tf_op | source)
XLA Modules:
  0.0 88.2 jit_solution(3159755720831059207)
XLA Ops:
  0.0 0.0 copy-start.1
  0.0 0.7 copy-done.1
  0.7 0.0 copy-start
  0.7 1.1 %copy-done = bf16[512,768]{1,0:T(8,128)(2,1)S(1)} copy-done((bf16[512,768]{1,0:T(8,128)(2,1)S(1)}, bf16[512,768]{1,0:T(8,128)(2,1)}, u32[]{:S(2)}) %copy-start) | copy-done | bytes 786456
  1.8 0.0 copy-start.2
  1.8 0.7 copy-done.2
  2.5 85.1 %shard_map.37 = f32[1,512]{1,0:T(1,128)S(1)} custom-call(s32[1,512]{1,0:T(1,128)S(1)} %bitcast.4, s32[1,512]{1,0:T(1,128)S(1)} %bitcast.5, bf16[512,768]{1,0:T(8,128)(2,1)S(1)} %copy-done), custom_call_target="tpu_custom_call" | custom-call | tf_op jit(solution)/shard_map/pallas_call | solution.py:487
  87.6 0.6 copy.5
Async XLA Ops:
  0.0 0.7 copy-start.1
  0.7 1.1 %copy-start = (bf16[512,768]{1,0:T(8,128)(2,1)S(1)}, bf16[512,768]{1,0:T(8,128)(2,1)}, u32[]{:S(2)}) copy-start(bf16[512,768]{1,0:T(8,128)(2,1)} %emb_hbm.1) | copy-start | bytes 2359300
  1.8 0.7 copy-start.2

commit v4 on v3

--- a/solution.py
+++ b/solution.py
@@ -27,10 +27,10 @@
     na, nx, home_hbm, cluster_hbm, emb_hbm, out_ref,
     home_ref, cluster_ref, emb_ref, unit, out1, in1, in2, sib_in, kept, acc, col,
     ids1, ids1_in, ids2, ids2_in, ids3_in, ids_sib, key_ids, row_ids,
-    den, den_in, ret, ret_in,
+    den, den_in, den_x, ret, ret_in,
     load, send1, recv1, send2, recv2, send3, recv3,
     isend1, irecv1, isend2, irecv2, isend3, irecv3, isend4, irecv4,
-    dsend1, drecv1, dsend2, drecv2,
+    dsend1, drecv1, dsend2, drecv2, dsend3, drecv3, entered,
 ):
     nb = na
     nk = 2 * nb // nx
@@ -69,11 +69,12 @@
 
     sibling = (shard + 1 - 2 * core, x)
 
-    def delta(t):
-        return ((t + 1) // 2 * (2 * (t % 2) - 1)) % na
-
-    ahead = [on(lax.rem(a + delta(t), na), b) for t in range(na)]
-    behind = [on(lax.rem(a + na - delta(t), na), b) for t in range(na)]
+    deltas = [0, 1, na - 1, na // 2]
+    for far in range(2, na // 2):
+        deltas += [far, na - far]
+
+    ahead = [on(lax.rem(a + d, na), b) for d in deltas]
+    behind = [on(lax.rem(a + na - d, na), b) for d in deltas]
     ring = [on(a, i) for i in range(nb)]
     b_to = [lax.rem(x - a - half * (k // nj) + nx + na * nx, nx) + nx * (k % nj) for k in range(nk)]
     owner = [on(a, b_to[k]) for k in range(nk)]
@@ -98,10 +99,10 @@
     def greet(device):
         pl.semaphore_signal(barrier, inc=1, device_id=device, device_id_type=MESH)
 
-    for j in range(nx):
-        for t in range(na):
-            if j + t > 0:
-                greet((ahead[t], right(j)))
+    for j in range(1, nx):
+        greet((shard, right(j)))
+    for t in range(1, na):
+        greet((ahead[t], x))
     for i in range(nb):
         @pl.when(b != i)
         def _():
@@ -121,12 +122,15 @@
     b_own = y_own + core * (z_own - y_own)
     x_own = (a_own + b_own + half * c_own) % nx
     k_own = c_own * nj + b_own // nx
-    step = (a_own - a + na) % na
-    step = jnp.where(step <= na // 2, jnp.maximum(2 * step - 1, 0), 2 * (na - step))
+    distance = (a_own - a + na) % na
+    step = jnp.zeros_like(distance)
+    for t in range(1, na):
+        step = jnp.where(distance == deltas[t], t, step)
     offset = (x_own - x + nx) % nx
     message = offset * na + step
     lane = k_own * CAP + pos
     slot = message * (nk * CAP) + lane
+    wide_lane = offset * (nk * CAP) + lane
 
     loads[2].wait()
     values = emb_ref[...].astype(F32)
@@ -137,12 +141,16 @@
     loads[1].wait()
     marks = (cluster_ref[...] + 1).astype(F32)
     in_step = (iota((na, rows), 0) == step).astype(BF16)
-    in_lane = jnp.where(iota((lanes, rows), 0) == offset * (nk * CAP) + lane, marks, 0.0)
+    in_lane = jnp.where(iota((lanes, rows), 0) == wide_lane, marks, 0.0)
     tags = nt_dot(in_step, in_lane.astype(BF16))
     for t in range(na):
         ids1[t] = tags[t : t + 1]
 
-    pl.semaphore_wait(barrier, na * nx - 1 + nb - 1 + 1)
+    pl.semaphore_wait(barrier, nx - 1 + na - 1 + nb - 1 + 1)
+    for j in range(1, nx):
+        pl.semaphore_signal(
+            entered, inc=1, device_id=(shard, right(j)), device_id_type=MESH
+        )
 
     def ids1_copy(t):
         return pltpu.make_async_remote_copy(
@@ -169,7 +177,7 @@
         q, sub = j * 2 + t // ns, t % ns
         return pltpu.make_async_remote_copy(
             src_ref=out1.at[q, sub], dst_ref=in1.at[q, sub],
-            send_sem=send1.at[j, t], recv_sem=recv1.at[j],
+            send_sem=send1.at[j, t], recv_sem=recv1.at[q],
             device_id=(ahead[t], right(j)), device_id_type=MESH,
         )
 
@@ -207,24 +215,20 @@
             device_id=(owner[k], x), device_id_type=MESH,
         )
 
-    def forward_stage(j):
-        for h in range(2):
-            q = j * 2 + h
-            for k in range(nk):
-                either(
-                    stays[k],
-                    lambda: pltpu.make_async_copy(
-                        in1.at[q, :, k], in2.at[q, b], recv2.at[q]
-                    ).start(),
-                    lambda: rows2_copy(q, k).start(),
-                )
-
-    def forwarded_stage(j):
+    def forward(q):
+        pltpu.make_async_copy(in1.at[q], in1.at[q], recv1.at[q]).wait()
+        for k in range(nk):
+            either(
+                stays[k],
+                lambda: pltpu.make_async_copy(in1.at[q, :, k], in2.at[q, b], recv2.at[q]).start(),
+                lambda: rows2_copy(q, k).start(),
+            )
+
+    def forwarded(q):
         for k in range(nk):
             @pl.when(jnp.logical_not(stays[k]))
             def _():
-                for h in range(2):
-                    rows2_copy(j * 2 + h, k).wait_send()
+                rows2_copy(q, k).wait_send()
 
     def sib_ids_copy():
         return pltpu.make_async_remote_copy(
@@ -284,15 +288,13 @@
                 sums += part
         return sums
 
-    def take(t, carry):
+    def pair_sums(t, carry):
         pltpu.make_async_copy(in2.at[t], in2.at[t], recv2.at[t]).wait()
         block = in2[t].reshape(nb * ns, 2 * CAP, hf).astype(F32)
         block = jnp.concatenate([block[:, :CAP, :], block[:, CAP:, :]], axis=2)
         kept[0, t] = block.reshape(chunk, feat).astype(BF16)
         sib_rows_copy(t).start()
-        return carry
-
-    def pair_sums(t, carry):
+
         groups = lax.div(t + group, group)
         sums = lax.fori_loop(
             0, groups, lambda g, c: tile(0, g, 0, t, t, True, True, c),
@@ -322,6 +324,7 @@
             lambda: pltpu.make_async_copy(ids2, ids2_in.at[b], irecv2).start(),
             lambda: ids2_copy(i).start(),
         )
+    pl.semaphore_wait(entered, nx - 1)
     send_stage(1, False)
     pltpu.make_async_copy(ids2_in, ids2_in, irecv2).wait()
     pltpu.make_async_copy(ids2_in, ids3_in.at[0], irecv3).start()
@@ -331,14 +334,12 @@
     def stage(j, carry):
         @pl.when(j < nx)
         def _():
-            here = in1.at[pl.ds(2 * j, 2)]
-            pltpu.make_async_copy(here, here, recv1.at[j]).wait()
-
-            @pl.when(j >= 2)
-            def _():
-                forwarded_stage(j - 2)
-
-            forward_stage(j)
+            for h in range(2):
+                @pl.when(j >= 2)
+                def _():
+                    forwarded(2 * j - 4 + h)
+
+                forward(2 * j + h)
 
             @pl.when(j < nx - 2)
             def _():
@@ -359,7 +360,6 @@
 
         @pl.when(computes & (j > 0))
         def _():
-            lax.fori_loop(2 * j - 2, 2 * j, take, 0)
             lax.fori_loop(2 * j - 2, 2 * j, pair_sums, 0)
         return carry
 
@@ -401,40 +401,52 @@
 
     for j in range(nx - 2, nx):
         sent_stage(j)
-        forwarded_stage(j)
     for i in range(1, na):
         ids1_copy(i).wait_send()
+    pltpu.make_async_copy(den_in, den_in, drecv1).wait()
+
+    def den2_copy(j):
+        return pltpu.make_async_remote_copy(
+            src_ref=den_in, dst_ref=den_x.at[j - 1],
+            send_sem=dsend2.at[j - 1], recv_sem=drecv2,
+            device_id=(shard, left(j)), device_id_type=MESH,
+        )
+
+    for j in range(1, nx):
+        den2_copy(j).start()
+    for q in range(2 * nx - 4, 2 * nx):
+        forwarded(q)
     for i in range(nb):
         @pl.when(b != i)
         def _():
             ids2_copy(i).wait_send()
     for j in range(1, nx):
         ids3_copy(j).wait_send()
-
-    at_lane = iota((nq, lanes), 1)
-
-    def shifted(block, source, target):
-        mine = jnp.where((at_lane >= source * CAP) & (at_lane < source * CAP + CAP), block, 0.0)
-        turns = ((target - source) * CAP) % lanes
-        return pltpu.roll(mine, turns, 1) if turns else mine
-
-    pltpu.make_async_copy(den_in, den_in, drecv1).wait()
-
-    def ret_copy(q, sub):
-        return pltpu.make_async_remote_copy(
-            src_ref=ret.at[q * ns + sub], dst_ref=ret_in.at[q * ns + sub],
-            send_sem=dsend2.at[q, sub], recv_sem=drecv2,
-            device_id=(behind[q % 2 * ns + sub], left(q // 2)), device_id_type=MESH,
-        )
-
+    pltpu.make_async_copy(den_x, den_x, drecv2).wait()
+
+    def ret_copy(t):
+        return pltpu.make_async_remote_copy(
+            src_ref=ret.at[t], dst_ref=ret_in.at[t],
+            send_sem=dsend3.at[t], recv_sem=drecv3,
+            device_id=(behind[t], x), device_id_type=MESH,
+        )
+
+    at_lane = iota((2, lanes), 1)
     for sub in range(ns):
-        block = functools.reduce(jnp.add, [shifted(den_in[k], sub, k) for k in range(nk)])
-        for q in range(nq):
-            ret[q * ns + sub] = block[q : q + 1]
-            if q + sub > 0:
-                ret_copy(q, sub).start()
+        block = jnp.zeros((2, lanes), F32)
+        for j in range(nx):
+            for k in range(nk):
+                part = den_in[k] if j == 0 else den_x[j - 1, k]
+                turns = ((j * nk + k - sub) * CAP) % lanes
+                part = jnp.where(at_lane // CAP == sub, part[2 * j : 2 * j + 2], 0.0)
+                block += pltpu.roll(part, turns, 1) if turns else part
+        for h in range(2):
+            t = h * ns + sub
+            ret[t] = block[h : h + 1]
+            if t > 0:
+                ret_copy(t).start()
             else:
-                pltpu.make_async_copy(ret.at[0], ret_in.at[0], drecv2).start()
+                pltpu.make_async_copy(ret.at[0], ret_in.at[0], drecv3).start()
 
     @pl.when(computes)
     def _():
@@ -446,13 +458,14 @@
             def _():
                 den1_copy(i).wait_send()
 
-    chosen = (iota((lanes, rows), 0) == message).astype(BF16)
-    pltpu.make_async_copy(ret, ret_in, drecv2).wait()
+    for j in range(1, nx):
+        den2_copy(j).wait_send()
+    chosen = (iota((lanes, rows), 0) == step).astype(BF16)
+    pltpu.make_async_copy(ret, ret_in, drecv3).wait()
 
     table = jnp.concatenate(
-        [ret_in[m] for m in range(na * nx)] + [jnp.zeros((lanes - na * nx, lanes), F32)], axis=0
-    )
-    table = table.T[: nk * CAP]
+        [ret_in[t] for t in range(na)] + [jnp.zeros((lanes - na, lanes), F32)], axis=0
+    ).T
     high = table.astype(BF16)
     rest = table - high.astype(F32)
     mid = rest.astype(BF16)
@@ -462,13 +475,11 @@
         + jnp.dot(mid, chosen, preferred_element_type=F32)
     ) + jnp.dot(high, chosen, preferred_element_type=F32)
     out_ref[...] = jnp.sum(
-        jnp.where(iota((nk * CAP, rows), 0) == lane, picked, 0.0), axis=0, keepdims=True
+        jnp.where(iota((lanes, rows), 0) == wide_lane, picked, 0.0), axis=0, keepdims=True
     )
 
-    for q in range(nq):
-        for sub in range(ns):
-            if q + sub > 0:
-                ret_copy(q, sub).wait_send()
+    for t in range(1, na):
+        ret_copy(t).wait_send()
 
 
 def shards(n_tile, embeddings, cluster, home):
@@ -481,7 +492,6 @@
     nq = 2 * nx
     chunk = na * ns * CAP
     hf = feat // 2
-    messages = na * nx
     vmem = pltpu.VMEM
     dma = pltpu.SemaphoreType.DMA
     out = pl.pallas_call(
@@ -511,12 +521,14 @@
             vmem((2, nq, chunk, 128), F32),
             vmem((na, nq, 128), F32),
             vmem((nk, nq, 128), F32),
-            vmem((messages, 1, 128), F32),
-            vmem((messages, 1, 128), F32),
+            vmem((nx - 1, nk, nq, 128), F32),
+            vmem((na, 1, 128), F32),
+            vmem((na, 1, 128), F32),
             dma((3,)),
-            dma((nx, na)), dma((nx,)), dma((nq, nk)), dma((nq,)), dma((nq,)), dma((nq,)),
+            dma((nx, na)), dma((nq,)), dma((nq, nk)), dma((nq,)), dma((nq,)), dma((nq,)),
             dma((na,)), dma(()), dma((na,)), dma(()), dma((nx,)), dma(()), dma(()), dma(()),
-            dma((na,)), dma(()), dma((nq, ns)), dma(()),
+            dma((na,)), dma(()), dma((nx - 1,)), dma(()), dma((na,)), dma(()),
+            pltpu.SemaphoreType.REGULAR,
         ],
         compiler_params=pltpu.CompilerParams(
             collective_id=0, has_side_effects=True, vmem_limit_bytes=48 * 2**20

time: 89 us -> 89.1 us (level)
  no operation moved by 1% of the time
where the time goes in v4:
time: 89.1 us; the launch traced here: 88.7 us
  Pallas kernels  85.6 us (96%)
  local copies, waits for them, and re-layouts  3.08 us (3%)
    pallas_call x1, Pallas kernels, shards(): pl.pallas_call(functools.partial(kernel, na, nx), out_shape=jax.ShapeDtyp...  85.6 us
    unnamed x7, local copies, waits for them, and re-layouts  3.08 us

profile of v4, /device:TPU:1, one launch (start us, length us, event | category | flops | bytes accessed | tf_op | source)
XLA Modules:
  0.0 88.7 jit_solution(6248277419809195120)
XLA Ops:
  0.0 0.0 copy-start.1
  0.0 0.7 copy-done.1
  0.7 0.0 copy-start
  0.7 1.1 %copy-done = bf16[512,768]{1,0:T(8,128)(2,1)S(1)} copy-done((bf16[512,768]{1,0:T(8,128)(2,1)S(1)}, bf16[512,768]{1,0:T(8,128)(2,1)}, u32[]{:S(2)}) %copy-start) | copy-done | bytes 786456
  1.8 0.0 copy-start.2
  1.8 0.7 copy-done.2
  2.5 85.6 %shard_map.37 = f32[1,512]{1,0:T(1,128)S(1)} custom-call(s32[1,512]{1,0:T(1,128)S(1)} %bitcast.4, s32[1,512]{1,0:T(1,128)S(1)} %bitcast.5, bf16[512,768]{1,0:T(8,128)(2,1)S(1)} %copy-done), custom_call_target="tpu_custom_call" | custom-call | tf_op jit(solution)/shard_map/pallas_call | solution.py:497
  88.1 0.6 copy.5
Async XLA Ops:
  0.0 0.7 copy-start.1
  0.7 1.1 %copy-start = (bf16[512,768]{1,0:T(8,128)(2,1)S(1)}, bf16[512,768]{1,0:T(8,128)(2,1)}, u32[]{:S(2)}) copy-start(bf16[512,768]{1,0:T(8,128)(2,1)} %emb_hbm.1) | copy-start | bytes 2359300
  1.8 0.7 copy-start.2

commit v5 on v4

--- a/solution.py
+++ b/solution.py
@@ -25,12 +25,12 @@
 
 def kernel(
     na, nx, home_hbm, cluster_hbm, emb_hbm, out_ref,
-    home_ref, cluster_ref, emb_ref, unit, out1, in1, in2, sib_in, kept, acc, col,
+    home_ref, cluster_ref, emb_ref, unit, out1, in1, in2, passing, sib_in, kept, acc, col,
     ids1, ids1_in, ids2, ids2_in, ids3_in, ids_sib, key_ids, row_ids,
-    den, den_in, den_x, ret, ret_in,
-    load, send1, recv1, send2, recv2, send3, recv3,
+    den, den_in, ret, ret_in,
+    load, send1, recv1, send2, recv2, send3, recv3, rsend, rrecv,
     isend1, irecv1, isend2, irecv2, isend3, irecv3, isend4, irecv4,
-    dsend1, drecv1, dsend2, drecv2, dsend3, drecv3, entered,
+    dsend1, drecv1, dsend2, drecv2, entered,
 ):
     nb = na
     nk = 2 * nb // nx
@@ -83,6 +83,12 @@
     computes = lax.rem(turn, half) == 0
     k_self = lax.div(turn, half) * nj + lax.div(b, nx)
     k_sib = lax.div(turn, half) * nj + lax.div(a, nx)
+
+    opposite = [computes & (b_to[k] == lax.rem(b + nb // 2, nb)) for k in range(nk)]
+    turned = 1 - 2 * lax.rem(b, 2)
+    relay = on(a, lax.rem(b - turned + nb, nb))
+    relay_from = lax.rem(b - turned + nb, nb)
+    relay_to = on(a, lax.rem(b + (nb // 2 - 1) * turned + nb, nb))
 
     def either(same, local, remote):
         pl.when(same)(local)
@@ -215,14 +221,39 @@
             device_id=(owner[k], x), device_id_type=MESH,
         )
 
-    def forward(q):
+    def forward(j, h):
+        q = 2 * j + h
         pltpu.make_async_copy(in1.at[q], in1.at[q], recv1.at[q]).wait()
         for k in range(nk):
+            def away(k=k):
+                if h == 0:
+                    rows2_copy(q, k).start()
+                else:
+                    either(
+                        opposite[k],
+                        lambda: relay_copy(j, k).start(),
+                        lambda: rows2_copy(q, k).start(),
+                    )
+
             either(
                 stays[k],
                 lambda: pltpu.make_async_copy(in1.at[q, :, k], in2.at[q, b], recv2.at[q]).start(),
-                lambda: rows2_copy(q, k).start(),
+                away,
             )
+
+    def relay_copy(j, k):
+        return pltpu.make_async_remote_copy(
+            src_ref=in1.at[2 * j + 1, :, k], dst_ref=passing.at[j],
+            send_sem=send2.at[2 * j + 1, k], recv_sem=rrecv.at[j],
+            device_id=(relay, x), device_id_type=MESH,
+        )
+
+    def passed_copy(j):
+        return pltpu.make_async_remote_copy(
+            src_ref=passing.at[j], dst_ref=in2.at[2 * j + 1, relay_from],
+            send_sem=rsend.at[j], recv_sem=recv2.at[2 * j + 1],
+            device_id=(relay_to, x), device_id_type=MESH,
+        )
 
     def forwarded(q):
         for k in range(nk):
@@ -339,12 +370,17 @@
                 def _():
                     forwarded(2 * j - 4 + h)
 
-                forward(2 * j + h)
+                forward(j, h)
 
             @pl.when(j < nx - 2)
             def _():
                 sent_stage(j)
                 send_stage(j + 2, False)
+
+            @pl.when(jnp.logical_not(computes))
+            def _():
+                pltpu.make_async_copy(passing.at[j], passing.at[j], rrecv.at[j]).wait()
+                passed_copy(j).start()
 
         @pl.when(computes & (j == 0))
         def _():
@@ -398,55 +434,45 @@
     @pl.when(jnp.logical_not(computes))
     def _():
         pltpu.make_async_copy(ids3_in, ids3_in, irecv3).wait()
+        for j in range(nx):
+            passed_copy(j).wait_send()
 
     for j in range(nx - 2, nx):
         sent_stage(j)
+    at_lane = iota((nq, lanes), 1)
+    in_place = [at_lane // CAP == sub for sub in range(ns)]
+    pltpu.make_async_copy(den_in, den_in, drecv1).wait()
+
+    def ret_copy(q, sub):
+        return pltpu.make_async_remote_copy(
+            src_ref=ret.at[q * ns + sub], dst_ref=ret_in.at[q * ns + sub],
+            send_sem=dsend2.at[q, sub], recv_sem=drecv2,
+            device_id=(behind[q % 2 * ns + sub], left(q // 2)), device_id_type=MESH,
+        )
+
+    for sub in range(ns):
+        block = jnp.zeros((nq, lanes), F32)
+        for k in range(nk):
+            part = jnp.where(in_place[sub], den_in[k], 0.0)
+            turns = ((k - sub) * CAP) % lanes
+            block += pltpu.roll(part, turns, 1) if turns else part
+        for q in range(nq):
+            ret[q * ns + sub] = block[q : q + 1]
+            if q + sub > 0:
+                ret_copy(q, sub).start()
+            else:
+                pltpu.make_async_copy(ret.at[0], ret_in.at[0], drecv2).start()
+
     for i in range(1, na):
         ids1_copy(i).wait_send()
-    pltpu.make_async_copy(den_in, den_in, drecv1).wait()
-
-    def den2_copy(j):
-        return pltpu.make_async_remote_copy(
-            src_ref=den_in, dst_ref=den_x.at[j - 1],
-            send_sem=dsend2.at[j - 1], recv_sem=drecv2,
-            device_id=(shard, left(j)), device_id_type=MESH,
-        )
-
-    for j in range(1, nx):
-        den2_copy(j).start()
-    for q in range(2 * nx - 4, 2 * nx):
-        forwarded(q)
     for i in range(nb):
         @pl.when(b != i)
         def _():
             ids2_copy(i).wait_send()
     for j in range(1, nx):
         ids3_copy(j).wait_send()
-    pltpu.make_async_copy(den_x, den_x, drecv2).wait()
-
-    def ret_copy(t):
-        return pltpu.make_async_remote_copy(
-            src_ref=ret.at[t], dst_ref=ret_in.at[t],
-            send_sem=dsend3.at[t], recv_sem=drecv3,
-            device_id=(behind[t], x), device_id_type=MESH,
-        )
-
-    at_lane = iota((2, lanes), 1)
-    for sub in range(ns):
-        block = jnp.zeros((2, lanes), F32)
-        for j in range(nx):
-            for k in range(nk):
-                part = den_in[k] if j == 0 else den_x[j - 1, k]
-                turns = ((j * nk + k - sub) * CAP) % lanes
-                part = jnp.where(at_lane // CAP == sub, part[2 * j : 2 * j + 2], 0.0)
-                block += pltpu.roll(part, turns, 1) if turns else part
-        for h in range(2):
-            t = h * ns + sub
-            ret[t] = block[h : h + 1]
-            if t > 0:
-                ret_copy(t).start()
-            else:
-                pltpu.make_async_copy(ret.at[0], ret_in.at[0], drecv3).start()
+    for q in range(2 * nx - 4, 2 * nx):
+        forwarded(q)
 
     @pl.when(computes)
     def _():
@@ -458,14 +484,13 @@
             def _():
                 den1_copy(i).wait_send()
 
-    for j in range(1, nx):
-        den2_copy(j).wait_send()
-    chosen = (iota((lanes, rows), 0) == step).astype(BF16)
-    pltpu.make_async_copy(ret, ret_in, drecv3).wait()
+    chosen = (iota((lanes, rows), 0) == message).astype(BF16)
+    pltpu.make_async_copy(ret, ret_in, drecv2).wait()
 
     table = jnp.concatenate(
-        [ret_in[t] for t in range(na)] + [jnp.zeros((lanes - na, lanes), F32)], axis=0
-    ).T
+        [ret_in[m] for m in range(na * nx)] + [jnp.zeros((lanes - na * nx, lanes), F32)], axis=0
+    )
+    table = table.T[: nk * CAP]
     high = table.astype(BF16)
     rest = table - high.astype(F32)
     mid = rest.astype(BF16)
@@ -475,11 +500,13 @@
         + jnp.dot(mid, chosen, preferred_element_type=F32)
     ) + jnp.dot(high, chosen, preferred_element_type=F32)
     out_ref[...] = jnp.sum(
-        jnp.where(iota((lanes, rows), 0) == wide_lane, picked, 0.0), axis=0, keepdims=True
+        jnp.where(iota((nk * CAP, rows), 0) == lane, picked, 0.0), axis=0, keepdims=True
     )
 
-    for t in range(1, na):
-        ret_copy(t).wait_send()
+    for q in range(nq):
+        for sub in range(ns):
+            if q + sub > 0:
+                ret_copy(q, sub).wait_send()
 
 
 def shards(n_tile, embeddings, cluster, home):
@@ -507,6 +534,7 @@
             vmem((nq, ns, nk, 2 * CAP, hf), BF16),
             vmem((nq, ns, nk, 2 * CAP, hf), BF16),
             vmem((nq, na, ns, 2 * CAP, hf), BF16),
+            vmem((nx, ns, 2 * CAP, hf), BF16),
             vmem((nq, chunk, feat), BF16),
             vmem((2, nq, chunk, feat), BF16),
             vmem((nq, chunk, 128), F32),
@@ -521,14 +549,13 @@
             vmem((2, nq, chunk, 128), F32),
             vmem((na, nq, 128), F32),
             vmem((nk, nq, 128), F32),
-            vmem((nx - 1, nk, nq, 128), F32),
-            vmem((na, 1, 128), F32),
-            vmem((na, 1, 128), F32),
+            vmem((na * nx, 1, 128), F32),
+            vmem((na * nx, 1, 128), F32),
             dma((3,)),
             dma((nx, na)), dma((nq,)), dma((nq, nk)), dma((nq,)), dma((nq,)), dma((nq,)),
+            dma((nx,)), dma((nx,)),
             dma((na,)), dma(()), dma((na,)), dma(()), dma((nx,)), dma(()), dma(()), dma(()),
-            dma((na,)), dma(()), dma((nx - 1,)), dma(()), dma((na,)), dma(()),
-            pltpu.SemaphoreType.REGULAR,
+            dma((na,)), dma(()), dma((nq, ns)), dma(()), pltpu.SemaphoreType.REGULAR,
         ],
         compiler_params=pltpu.CompilerParams(
             collective_id=0, has_side_effects=True, vmem_limit_bytes=48 * 2**20

time: 89.1 us -> 85.4 us (0.958)
  Pallas kernels: 85.6 us -> 81.9 us
    pallas_call x1, Pallas kernels: 85.6 us -> 81.9 us  [shards(): pl.pallas_call(functools.partial(kernel, na, nx), out_shape=jax.ShapeDtyp...]
where the time goes in v5:
time: 85.4 us; the launch traced here: 85 us
  Pallas kernels  81.9 us (96%)
  local copies, waits for them, and re-layouts  3.08 us (4%)
    pallas_call x1, Pallas kernels, shards(): pl.pallas_call(functools.partial(kernel, na, nx), out_shape=jax.ShapeDtyp...  81.9 us
    unnamed x7, local copies, waits for them, and re-layouts  3.08 us

profile of v5, /device:TPU:1, one launch (start us, length us, event | category | flops | bytes accessed | tf_op | source)
XLA Modules:
  0.0 85.0 jit_solution(8181447322979742553)
XLA Ops:
  0.0 0.0 copy-start.1
  0.0 0.7 copy-done.1
  0.7 0.0 copy-start
  0.7 1.1 %copy-done = bf16[512,768]{1,0:T(8,128)(2,1)S(1)} copy-done((bf16[512,768]{1,0:T(8,128)(2,1)S(1)}, bf16[512,768]{1,0:T(8,128)(2,1)}, u32[]{:S(2)}) %copy-start) | copy-done | bytes 786456
  1.8 0.0 copy-start.2
  1.8 0.7 copy-done.2
  2.5 81.9 %shard_map.37 = f32[1,512]{1,0:T(1,128)S(1)} custom-call(s32[1,512]{1,0:T(1,128)S(1)} %bitcast.4, s32[1,512]{1,0:T(1,128)S(1)} %bitcast.5, bf16[512,768]{1,0:T(8,128)(2,1)S(1)} %copy-done), custom_call_target="tpu_custom_call" | custom-call | tf_op jit(solution)/shard_map/pallas_call | solution.py:524
  84.4 0.6 copy.5
Async XLA Ops:
  0.0 0.7 copy-start.1
  0.7 1.1 %copy-start = (bf16[512,768]{1,0:T(8,128)(2,1)S(1)}, bf16[512,768]{1,0:T(8,128)(2,1)}, u32[]{:S(2)}) copy-start(bf16[512,768]{1,0:T(8,128)(2,1)} %emb_hbm.1) | copy-start | bytes 2359300
  1.8 0.7 copy-start.2

commit v6 on v5

--- a/solution.py
+++ b/solution.py
@@ -25,7 +25,7 @@
 
 def kernel(
     na, nx, home_hbm, cluster_hbm, emb_hbm, out_ref,
-    home_ref, cluster_ref, emb_ref, unit, out1, in1, in2, passing, sib_in, kept, acc, col,
+    home_ref, cluster_ref, emb_ref, unit, out1, in1, in2, passing, sib_in, kept, acc, col, col_part,
     ids1, ids1_in, ids2, ids2_in, ids3_in, ids_sib, key_ids, row_ids,
     den, den_in, ret, ret_in,
     load, send1, recv1, send2, recv2, send3, recv3, rsend, rrecv,
@@ -43,7 +43,6 @@
     chunk = nb * ns * CAP
     wide = ns * CAP
     lanes = 128
-    group = 4
 
     loads = [
         pltpu.make_async_copy(src, dst, load.at[i])
@@ -152,41 +151,6 @@
     for t in range(na):
         ids1[t] = tags[t : t + 1]
 
-    pl.semaphore_wait(barrier, nx - 1 + na - 1 + nb - 1 + 1)
-    for j in range(1, nx):
-        pl.semaphore_signal(
-            entered, inc=1, device_id=(shard, right(j)), device_id_type=MESH
-        )
-
-    def ids1_copy(t):
-        return pltpu.make_async_remote_copy(
-            src_ref=ids1.at[t], dst_ref=ids1_in.at[t],
-            send_sem=isend1.at[t], recv_sem=irecv1,
-            device_id=(ahead[t], x), device_id_type=MESH,
-        )
-
-    def ids2_copy(i):
-        return pltpu.make_async_remote_copy(
-            src_ref=ids2, dst_ref=ids2_in.at[b],
-            send_sem=isend2.at[i], recv_sem=irecv2,
-            device_id=(ring[i], x), device_id_type=MESH,
-        )
-
-    def ids3_copy(j):
-        return pltpu.make_async_remote_copy(
-            src_ref=ids2_in, dst_ref=ids3_in.at[j],
-            send_sem=isend3.at[j], recv_sem=irecv3,
-            device_id=(shard, right(j)), device_id_type=MESH,
-        )
-
-    def out1_copy(j, t):
-        q, sub = j * 2 + t // ns, t % ns
-        return pltpu.make_async_remote_copy(
-            src_ref=out1.at[q, sub], dst_ref=in1.at[q, sub],
-            send_sem=send1.at[j, t], recv_sem=recv1.at[q],
-            device_id=(ahead[t], right(j)), device_id_type=MESH,
-        )
-
     def place(j, h):
         q = j * 2 + h
         size = ns * nk * CAP
@@ -196,9 +160,48 @@
         placed = jnp.concatenate([placed[:, :, :hf], placed[:, :, hf:]], axis=1).astype(BF16)
         out1[q] = placed.reshape(ns, nk, 2 * CAP, hf)
 
+    for h in range(2):
+        place(0, h)
+
+    pl.semaphore_wait(barrier, nx - 1 + na - 1 + nb - 1 + 1)
+    for j in range(1, nx):
+        pl.semaphore_signal(
+            entered, inc=1, device_id=(shard, right(j)), device_id_type=MESH
+        )
+
+    def ids1_copy(t):
+        return pltpu.make_async_remote_copy(
+            src_ref=ids1.at[t], dst_ref=ids1_in.at[t],
+            send_sem=isend1.at[t], recv_sem=irecv1,
+            device_id=(ahead[t], x), device_id_type=MESH,
+        )
+
+    def ids2_copy(i):
+        return pltpu.make_async_remote_copy(
+            src_ref=ids2, dst_ref=ids2_in.at[b],
+            send_sem=isend2.at[i], recv_sem=irecv2,
+            device_id=(ring[i], x), device_id_type=MESH,
+        )
+
+    def ids3_copy(j):
+        return pltpu.make_async_remote_copy(
+            src_ref=ids2_in, dst_ref=ids3_in.at[j],
+            send_sem=isend3.at[j], recv_sem=irecv3,
+            device_id=(shard, right(j)), device_id_type=MESH,
+        )
+
+    def out1_copy(j, t):
+        q, sub = j * 2 + t // ns, t % ns
+        return pltpu.make_async_remote_copy(
+            src_ref=out1.at[q, sub], dst_ref=in1.at[q, sub],
+            send_sem=send1.at[j, t], recv_sem=recv1.at[q],
+            device_id=(ahead[t], right(j)), device_id_type=MESH,
+        )
+
     def send_stage(j, first):
         for h in range(2):
-            place(j, h)
+            if not first:
+                place(j, h)
             for t in range(h * ns, (h + 1) * ns):
                 if first and t == 0:
                     pltpu.make_async_copy(out1.at[0, 0], in1.at[0, 0], recv1.at[0]).start()
@@ -292,19 +295,19 @@
 
         lax.fori_loop(0, nq, spread, 0)
 
-    def tile(side, g, key_side, t, last, by_row, by_col, sums):
-        left = kept[side, pl.ds(g * group, group)].reshape(group * chunk, feat)
+    def tile(size, side, key_side, t, last, by_row, by_col):
+        left = kept[side, :size].reshape(size * chunk, feat)
         scores = nt_dot(left, kept[key_side, t])
         weights = jnp.exp2(scores * SCALE)
         theirs = key_ids[key_side, t, 0:1, :]
-        for i in range(group):
-            at = g * group + i
+        sums = jnp.zeros((8, chunk), F32)
+        for at in range(size):
             mine = row_ids[side, at]
             valid = jnp.where(at <= last, theirs, -1.0)
             matched = [
                 jnp.where(
                     mine == valid[:, j : j + lanes],
-                    weights[i * chunk : (i + 1) * chunk, j : j + lanes],
+                    weights[at * chunk : (at + 1) * chunk, j : j + lanes],
                     0.0,
                 )
                 for j in range(0, chunk, lanes)
@@ -317,7 +320,15 @@
                 if by_row:
                     part = jnp.where(at < t, part, 0.0)
                 sums += part
-        return sums
+        if by_col:
+            col_part[...] += sums
+
+    def strip(side, key_side, t, last, by_row, by_col):
+        either(
+            last < nq // 2,
+            lambda: tile(nq // 2, side, key_side, t, last, by_row, by_col),
+            lambda: tile(nq, side, key_side, t, last, by_row, by_col),
+        )
 
     def pair_sums(t, carry):
         pltpu.make_async_copy(in2.at[t], in2.at[t], recv2.at[t]).wait()
@@ -326,21 +337,13 @@
         kept[0, t] = block.reshape(chunk, feat).astype(BF16)
         sib_rows_copy(t).start()
 
-        groups = lax.div(t + group, group)
-        sums = lax.fori_loop(
-            0, groups, lambda g, c: tile(0, g, 0, t, t, True, True, c),
-            jnp.zeros((8, chunk), F32),
-        )
+        col_part[...] = jnp.zeros_like(col_part)
+        strip(0, 0, t, t, True, True)
         sib_rows_copy(t).wait_recv()
         kept[1, t] = sib_in[t]
-        sums = lax.fori_loop(
-            0, groups, lambda g, c: tile(1, g, 0, t, t, False, True, c), sums
-        )
-        col[pl.ds(t, 1), :] = jnp.sum(sums, axis=0, keepdims=True)
-        lax.fori_loop(
-            0, lax.div(t + group - 1, group),
-            lambda g, c: tile(0, g, 1, t, t - 1, True, False, c), 0,
-        )
+        strip(1, 0, t, t, False, True)
+        col[pl.ds(t, 1), :] = jnp.sum(col_part[...], axis=0, keepdims=True)
+        pl.when(t > 0)(lambda: strip(0, 1, t, t - 1, True, False))
         return carry
 
     pltpu.make_async_copy(ids1.at[0], ids1_in.at[0], irecv1).start()
@@ -357,10 +360,6 @@
         )
     pl.semaphore_wait(entered, nx - 1)
     send_stage(1, False)
-    pltpu.make_async_copy(ids2_in, ids2_in, irecv2).wait()
-    pltpu.make_async_copy(ids2_in, ids3_in.at[0], irecv3).start()
-    for j in range(1, nx):
-        ids3_copy(j).start()
 
     def stage(j, carry):
         @pl.when(j < nx)
@@ -372,6 +371,13 @@
 
                 forward(j, h)
 
+            @pl.when(j == 0)
+            def _():
+                pltpu.make_async_copy(ids2_in, ids2_in, irecv2).wait()
+                pltpu.make_async_copy(ids2_in, ids3_in.at[0], irecv3).start()
+                for i in range(1, nx):
+                    ids3_copy(i).start()
+
             @pl.when(j < nx - 2)
             def _():
                 sent_stage(j)
@@ -382,15 +388,12 @@
                 pltpu.make_async_copy(passing.at[j], passing.at[j], rrecv.at[j]).wait()
                 passed_copy(j).start()
 
-        @pl.when(computes & (j == 0))
+        @pl.when(computes & (j == 1))
         def _():
             pltpu.make_async_copy(ids3_in, ids3_in, irecv3).wait()
             sib_ids_copy().start()
             spread_ids(ids3_in, 0, k_self)
             acc[...] = jnp.zeros_like(acc)
-
-        @pl.when(computes & (j == 1))
-        def _():
             sib_ids_copy().wait_recv()
             spread_ids(ids_sib, 1, k_sib)
 
@@ -401,11 +404,11 @@
 
     lax.fori_loop(0, nx + 1, stage, 0)
 
-    def den1_copy(to):
-        return pltpu.make_async_remote_copy(
-            src_ref=den.at[to], dst_ref=den_in.at[k_self],
-            send_sem=dsend1.at[to], recv_sem=drecv1,
-            device_id=(ring[to], x), device_id_type=MESH,
+    def den1_copy(to, u):
+        return pltpu.make_async_remote_copy(
+            src_ref=den.at[to], dst_ref=den_in.at[u, k_self],
+            send_sem=dsend1.at[to, u], recv_sem=drecv1,
+            device_id=(ring[to], left(2 * u)), device_id_type=MESH,
         )
 
     @pl.when(computes)
@@ -427,9 +430,10 @@
             den[j] = (den[j] + part) * (2.0 ** (-SCALE))
             either(
                 b == j,
-                lambda: pltpu.make_async_copy(den.at[j], den_in.at[k_self], drecv1).start(),
-                lambda: den1_copy(j).start(),
+                lambda: pltpu.make_async_copy(den.at[j], den_in.at[0, k_self], drecv1).start(),
+                lambda: den1_copy(j, 0).start(),
             )
+            den1_copy(j, 1).start()
 
     @pl.when(jnp.logical_not(computes))
     def _():
@@ -443,25 +447,29 @@
     in_place = [at_lane // CAP == sub for sub in range(ns)]
     pltpu.make_async_copy(den_in, den_in, drecv1).wait()
 
-    def ret_copy(q, sub):
-        return pltpu.make_async_remote_copy(
-            src_ref=ret.at[q * ns + sub], dst_ref=ret_in.at[q * ns + sub],
-            send_sem=dsend2.at[q, sub], recv_sem=drecv2,
-            device_id=(behind[q % 2 * ns + sub], left(q // 2)), device_id_type=MESH,
+    def ret_copy(v, t):
+        return pltpu.make_async_remote_copy(
+            src_ref=ret.at[v * na + t], dst_ref=ret_in.at[v * na + t],
+            send_sem=dsend2.at[v, t], recv_sem=drecv2,
+            device_id=(behind[t], left(v)), device_id_type=MESH,
         )
 
     for sub in range(ns):
-        block = jnp.zeros((nq, lanes), F32)
-        for k in range(nk):
-            part = jnp.where(in_place[sub], den_in[k], 0.0)
-            turns = ((k - sub) * CAP) % lanes
-            block += pltpu.roll(part, turns, 1) if turns else part
-        for q in range(nq):
-            ret[q * ns + sub] = block[q : q + 1]
-            if q + sub > 0:
-                ret_copy(q, sub).start()
-            else:
-                pltpu.make_async_copy(ret.at[0], ret_in.at[0], drecv2).start()
+        blocks = [jnp.zeros((nq, lanes), F32)] * 2
+        for u in range(2):
+            for k in range(nk):
+                part = jnp.where(in_place[sub], den_in[u, k], 0.0)
+                turns = ((u * nk + k - sub) * CAP) % lanes
+                blocks[u] += pltpu.roll(part, turns, 1) if turns else part
+        for v in range(2):
+            for h in range(2):
+                t = h * ns + sub
+                at = 2 * v + h
+                ret[v * na + t] = blocks[0][at : at + 1] + blocks[1][at + 4 : at + 5]
+                if v + t > 0:
+                    ret_copy(v, t).start()
+                else:
+                    pltpu.make_async_copy(ret.at[0], ret_in.at[0], drecv2).start()
 
     for i in range(1, na):
         ids1_copy(i).wait_send()
@@ -482,15 +490,17 @@
         for i in range(nb):
             @pl.when(b != i)
             def _():
-                den1_copy(i).wait_send()
-
-    chosen = (iota((lanes, rows), 0) == message).astype(BF16)
+                den1_copy(i, 0).wait_send()
+
+            den1_copy(i, 1).wait_send()
+
+    chosen = (iota((lanes, rows), 0) == offset % 2 * na + step).astype(BF16)
     pltpu.make_async_copy(ret, ret_in, drecv2).wait()
 
     table = jnp.concatenate(
-        [ret_in[m] for m in range(na * nx)] + [jnp.zeros((lanes - na * nx, lanes), F32)], axis=0
+        [ret_in[m] for m in range(2 * na)] + [jnp.zeros((lanes - 2 * na, lanes), F32)], axis=0
     )
-    table = table.T[: nk * CAP]
+    table = table.T[: 2 * nk * CAP]
     high = table.astype(BF16)
     rest = table - high.astype(F32)
     mid = rest.astype(BF16)
@@ -500,13 +510,14 @@
         + jnp.dot(mid, chosen, preferred_element_type=F32)
     ) + jnp.dot(high, chosen, preferred_element_type=F32)
     out_ref[...] = jnp.sum(
-        jnp.where(iota((nk * CAP, rows), 0) == lane, picked, 0.0), axis=0, keepdims=True
+        jnp.where(iota((2 * nk * CAP, rows), 0) == offset // 2 * (nk * CAP) + lane, picked, 0.0),
+        axis=0, keepdims=True,
     )
 
-    for q in range(nq):
-        for sub in range(ns):
-            if q + sub > 0:
-                ret_copy(q, sub).wait_send()
+    for v in range(2):
+        for t in range(na):
+            if v + t > 0:
+                ret_copy(v, t).wait_send()
 
 
 def shards(n_tile, embeddings, cluster, home):
@@ -539,6 +550,7 @@
             vmem((2, nq, chunk, feat), BF16),
             vmem((nq, chunk, 128), F32),
             vmem((nq, chunk), F32),
+            vmem((8, chunk), F32),
             vmem((na, 1, 128), F32),
             vmem((na, 1, 128), F32),
             vmem((na, 128), F32),
@@ -548,14 +560,14 @@
             vmem((2, nq, 8, chunk), F32),
             vmem((2, nq, chunk, 128), F32),
             vmem((na, nq, 128), F32),
-            vmem((nk, nq, 128), F32),
-            vmem((na * nx, 1, 128), F32),
-            vmem((na * nx, 1, 128), F32),
+            vmem((2, nk, nq, 128), F32),
+            vmem((2 * na, 1, 128), F32),
+            vmem((2 * na, 1, 128), F32),
             dma((3,)),
             dma((nx, na)), dma((nq,)), dma((nq, nk)), dma((nq,)), dma((nq,)), dma((nq,)),
             dma((nx,)), dma((nx,)),
             dma((na,)), dma(()), dma((na,)), dma(()), dma((nx,)), dma(()), dma(()), dma(()),
-            dma((na,)), dma(()), dma((nq, ns)), dma(()), pltpu.SemaphoreType.REGULAR,
+            dma((na, 2)), dma(()), dma((2, na)), dma(()), pltpu.SemaphoreType.REGULAR,
         ],
         compiler_params=pltpu.CompilerParams(
             collective_id=0, has_side_effects=True, vmem_limit_bytes=48 * 2**20

time: 85.4 us -> 80.7 us (0.945)
  Pallas kernels: 81.9 us -> 76.7 us
    pallas_call x1, Pallas kernels: 81.9 us -> 76.7 us  [shards(): pl.pallas_call(functools.partial(kernel, na, nx), out_shape=jax.ShapeDtyp...]
where the time goes in v6:
time: 80.7 us; the launch traced here: 79.8 us
  Pallas kernels  76.7 us (95%)
  local copies, waits for them, and re-layouts  3.08 us (4%)
    pallas_call x1, Pallas kernels, shards(): pl.pallas_call(functools.partial(kernel, na, nx), out_shape=jax.ShapeDtyp...  76.7 us
    unnamed x7, local copies, waits for them, and re-layouts  3.08 us

profile of v6, /device:TPU:1, one launch (start us, length us, event | category | flops | bytes accessed | tf_op | source)
XLA Modules:
  0.0 79.8 jit_solution(7820516176540866439)
XLA Ops:
  0.0 0.0 copy-start.1
  0.0 0.7 copy-done.1
  0.7 0.0 copy-start
  0.7 1.1 %copy-done = bf16[512,768]{1,0:T(8,128)(2,1)S(1)} copy-done((bf16[512,768]{1,0:T(8,128)(2,1)S(1)}, bf16[512,768]{1,0:T(8,128)(2,1)}, u32[]{:S(2)}) %copy-start) | copy-done | bytes 786456
  1.8 0.0 copy-start.2
  1.8 0.7 copy-done.2
  2.5 76.7 %shard_map.37 = f32[1,512]{1,0:T(1,128)S(1)} custom-call(s32[1,512]{1,0:T(1,128)S(1)} %bitcast.4, s32[1,512]{1,0:T(1,128)S(1)} %bitcast.5, bf16[512,768]{1,0:T(8,128)(2,1)S(1)} %copy-done), custom_call_target="tpu_custom_call" | custom-call | tf_op jit(solution)/shard_map/pallas_call | solution.py:535
  79.2 0.6 copy.5
Async XLA Ops:
  0.0 0.7 copy-start.1
  0.7 1.1 %copy-start = (bf16[512,768]{1,0:T(8,128)(2,1)S(1)}, bf16[512,768]{1,0:T(8,128)(2,1)}, u32[]{:S(2)}) copy-start(bf16[512,768]{1,0:T(8,128)(2,1)} %emb_hbm.1) | copy-start | bytes 2359300
  1.8 0.7 copy-start.2

commit v7 on v6

--- a/solution.py
+++ b/solution.py
@@ -25,12 +25,12 @@
 
 def kernel(
     na, nx, home_hbm, cluster_hbm, emb_hbm, out_ref,
-    home_ref, cluster_ref, emb_ref, unit, out1, in1, in2, passing, sib_in, kept, acc, col, col_part,
+    home_ref, cluster_ref, emb_ref, unit, out1, in1, in2, passing, sib_in, kept, acc, col, col_part, den_out, den_sib,
     ids1, ids1_in, ids2, ids2_in, ids3_in, ids_sib, key_ids, row_ids,
     den, den_in, ret, ret_in,
     load, send1, recv1, send2, recv2, send3, recv3, rsend, rrecv,
     isend1, irecv1, isend2, irecv2, isend3, irecv3, isend4, irecv4,
-    dsend1, drecv1, dsend2, drecv2, entered,
+    dsend1, drecv1, dsend2, drecv2, dsend3, drecv3, entered,
 ):
     nb = na
     nk = 2 * nb // nx
@@ -290,16 +290,17 @@
             row_ids[side, q] = jnp.broadcast_to(
                 jnp.sum(block, axis=1, keepdims=True), (chunk, lanes)
             )
-            key_ids[side, q] = nt_dot(jnp.ones((8, lanes), BF16), block.astype(BF16))
+            if side == 0:
+                key_ids[q] = nt_dot(jnp.ones((8, lanes), BF16), block.astype(BF16))
             return carry
 
         lax.fori_loop(0, nq, spread, 0)
 
-    def tile(size, side, key_side, t, last, by_row, by_col):
+    def tile(size, side, t, last):
         left = kept[side, :size].reshape(size * chunk, feat)
-        scores = nt_dot(left, kept[key_side, t])
+        scores = nt_dot(left, kept[0, t])
         weights = jnp.exp2(scores * SCALE)
-        theirs = key_ids[key_side, t, 0:1, :]
+        theirs = key_ids[t, 0:1, :]
         sums = jnp.zeros((8, chunk), F32)
         for at in range(size):
             mine = row_ids[side, at]
@@ -312,22 +313,21 @@
                 )
                 for j in range(0, chunk, lanes)
             ]
-            if by_row:
-                acc[at] += functools.reduce(jnp.add, matched)
-            if by_col:
-                parts = [jnp.sum(m.reshape(chunk // 8, 8, lanes), axis=0) for m in matched]
-                part = jnp.concatenate(parts, axis=1)
-                if by_row:
-                    part = jnp.where(at < t, part, 0.0)
-                sums += part
-        if by_col:
-            col_part[...] += sums
-
-    def strip(side, key_side, t, last, by_row, by_col):
+            acc[side, at] += functools.reduce(jnp.add, matched)
+            parts = [jnp.sum(m.reshape(chunk // 8, 8, lanes), axis=0) for m in matched]
+            part = jnp.concatenate(parts, axis=1)
+            sums += jnp.where(at < t, part, 0.0) if side == 0 else part
+        col_part[...] += sums
+
+    def strip(side, t, last):
         either(
             last < nq // 2,
-            lambda: tile(nq // 2, side, key_side, t, last, by_row, by_col),
-            lambda: tile(nq, side, key_side, t, last, by_row, by_col),
+            lambda: tile(nq // 2, side, t, last),
+            lambda: either(
+                last < nq // 4 * 3,
+                lambda: tile(nq // 4 * 3, side, t, last),
+                lambda: tile(nq, side, t, last),
+            ),
         )
 
     def pair_sums(t, carry):
@@ -338,12 +338,11 @@
         sib_rows_copy(t).start()
 
         col_part[...] = jnp.zeros_like(col_part)
-        strip(0, 0, t, t, True, True)
+        strip(0, t, t)
         sib_rows_copy(t).wait_recv()
         kept[1, t] = sib_in[t]
-        strip(1, 0, t, t, False, True)
+        strip(1, t, t - core)
         col[pl.ds(t, 1), :] = jnp.sum(col_part[...], axis=0, keepdims=True)
-        pl.when(t > 0)(lambda: strip(0, 1, t, t - 1, True, False))
         return carry
 
     pltpu.make_async_copy(ids1.at[0], ids1_in.at[0], irecv1).start()
@@ -404,6 +403,12 @@
 
     lax.fori_loop(0, nx + 1, stage, 0)
 
+    def sib_den_copy():
+        return pltpu.make_async_remote_copy(
+            src_ref=den_out, dst_ref=den_sib, send_sem=dsend3, recv_sem=drecv3,
+            device_id=sibling, device_id_type=MESH,
+        )
+
     def den1_copy(to, u):
         return pltpu.make_async_remote_copy(
             src_ref=den.at[to], dst_ref=den_in.at[u, k_self],
@@ -414,20 +419,24 @@
     @pl.when(computes)
     def _():
         same = iota((chunk, lanes), 1) == iota((chunk, lanes), 0) % wide
-        for t in range(nq):
-            sums = jnp.sum(acc[t], axis=1, keepdims=True)
-            block = jnp.where(same, sums, 0.0).reshape(nb, wide, lanes)
-            block = jnp.sum(block, axis=1)
-            for j in range(nb):
-                den[j, t : t + 1, :] = block[j : j + 1]
+        for side, result in ((1, den_out), (0, den)):
+            for t in range(nq):
+                sums = jnp.sum(acc[side, t], axis=1, keepdims=True)
+                block = jnp.where(same, sums, 0.0).reshape(nb, wide, lanes)
+                block = jnp.sum(block, axis=1)
+                for j in range(nb):
+                    result[j, t : t + 1, :] = block[j : j + 1]
+            if side == 1:
+                sib_den_copy().start()
         by_col = col[...]
         per = lanes // wide
+        sib_den_copy().wait_recv()
         for j in range(nb):
             part = by_col[:, j // per * lanes : (j // per + 1) * lanes]
             turns = (-(j % per) * wide) % lanes
             part = pltpu.roll(part, turns, 1) if turns else part
             part = jnp.where(iota((nq, lanes), 1) < wide, part, 0.0)
-            den[j] = (den[j] + part) * (2.0 ** (-SCALE))
+            den[j] = (den[j] + part + den_sib[j]) * (2.0 ** (-SCALE))
             either(
                 b == j,
                 lambda: pltpu.make_async_copy(den.at[j], den_in.at[0, k_self], drecv1).start(),
@@ -485,6 +494,7 @@
     @pl.when(computes)
     def _():
         sib_ids_copy().wait_send()
+        sib_den_copy().wait_send()
         for q in range(nq):
             sib_rows_copy(q).wait_send()
         for i in range(nb):
@@ -548,16 +558,18 @@
             vmem((nx, ns, 2 * CAP, hf), BF16),
             vmem((nq, chunk, feat), BF16),
             vmem((2, nq, chunk, feat), BF16),
-            vmem((nq, chunk, 128), F32),
+            vmem((2, nq, chunk, 128), F32),
             vmem((nq, chunk), F32),
             vmem((8, chunk), F32),
+            vmem((na, nq, 128), F32),
+            vmem((na, nq, 128), F32),
             vmem((na, 1, 128), F32),
             vmem((na, 1, 128), F32),
             vmem((na, 128), F32),
             vmem((na, na, 128), F32),
             vmem((nx, na, na, 128), F32),
             vmem((nx, na, na, 128), F32),
-            vmem((2, nq, 8, chunk), F32),
+            vmem((nq, 8, chunk), F32),
             vmem((2, nq, chunk, 128), F32),
             vmem((na, nq, 128), F32),
             vmem((2, nk, nq, 128), F32),
@@ -567,7 +579,8 @@
             dma((nx, na)), dma((nq,)), dma((nq, nk)), dma((nq,)), dma((nq,)), dma((nq,)),
             dma((nx,)), dma((nx,)),
             dma((na,)), dma(()), dma((na,)), dma(()), dma((nx,)), dma(()), dma(()), dma(()),
-            dma((na, 2)), dma(()), dma((2, na)), dma(()), pltpu.SemaphoreType.REGULAR,
+            dma((na, 2)), dma(()), dma((2, na)), dma(()), dma(()), dma(()),
+            pltpu.SemaphoreType.REGULAR,
         ],
         compiler_params=pltpu.CompilerParams(
             collective_id=0, has_side_effects=True, vmem_limit_bytes=48 * 2**20

time: 80.7 us -> 79 us (0.979)
  Pallas kernels: 76.7 us -> 74.9 us
    pallas_call x1, Pallas kernels: 76.7 us -> 74.9 us  [shards(): pl.pallas_call(functools.partial(kernel, na, nx), out_shape=jax.ShapeDtyp...]
where the time goes in v7:
time: 79 us; the launch traced here: 78 us
  Pallas kernels  74.9 us (95%)
  local copies, waits for them, and re-layouts  3.08 us (4%)
    pallas_call x1, Pallas kernels, shards(): pl.pallas_call(functools.partial(kernel, na, nx), out_shape=jax.ShapeDtyp...  74.9 us
    unnamed x7, local copies, waits for them, and re-layouts  3.08 us

profile of v7, /device:TPU:1, one launch (start us, length us, event | category | flops | bytes accessed | tf_op | source)
XLA Modules:
  0.0 78.0 jit_solution(14324661948666181158)
XLA Ops:
  0.0 0.0 copy-start.1
  0.0 0.7 copy-done.1
  0.7 0.0 copy-start
  0.7 1.1 %copy-done = bf16[512,768]{1,0:T(8,128)(2,1)S(1)} copy-done((bf16[512,768]{1,0:T(8,128)(2,1)S(1)}, bf16[512,768]{1,0:T(8,128)(2,1)}, u32[]{:S(2)}) %copy-start) | copy-done | bytes 786456
  1.8 0.0 copy-start.2
  1.8 0.7 copy-done.2
  2.5 74.9 %shard_map.37 = f32[1,512]{1,0:T(1,128)S(1)} custom-call(s32[1,512]{1,0:T(1,128)S(1)} %bitcast.4, s32[1,512]{1,0:T(1,128)S(1)} %bitcast.5, bf16[512,768]{1,0:T(8,128)(2,1)S(1)} %copy-done), custom_call_target="tpu_custom_call" | custom-call | tf_op jit(solution)/shard_map/pallas_call | solution.py:545
  77.4 0.6 copy.5
Async XLA Ops:
  0.0 0.7 copy-start.1
  0.7 1.1 %copy-start = (bf16[512,768]{1,0:T(8,128)(2,1)S(1)}, bf16[512,768]{1,0:T(8,128)(2,1)}, u32[]{:S(2)}) copy-start(bf16[512,768]{1,0:T(8,128)(2,1)} %emb_hbm.1) | copy-start | bytes 2359300
  1.8 0.7 copy-start.2

commit v8 on v7

--- a/solution.py
+++ b/solution.py
@@ -320,15 +320,10 @@
         col_part[...] += sums
 
     def strip(side, t, last):
-        either(
-            last < nq // 2,
-            lambda: tile(nq // 2, side, t, last),
-            lambda: either(
-                last < nq // 4 * 3,
-                lambda: tile(nq // 4 * 3, side, t, last),
-                lambda: tile(nq, side, t, last),
-            ),
-        )
+        for size in range(2, nq + 1, 2):
+            @pl.when((last >= size - 2) & (last < size))
+            def _():
+                tile(size, side, t, last)
 
     def pair_sums(t, carry):
         pltpu.make_async_copy(in2.at[t], in2.at[t], recv2.at[t]).wait()

time: 79 us -> 78.5 us (level)
  no operation moved by 1% of the time
where the time goes in v8:
time: 78.5 us; the launch traced here: 77.4 us
  Pallas kernels  74.3 us (95%)
  local copies, waits for them, and re-layouts  3.08 us (4%)
    pallas_call x1, Pallas kernels, shards(): pl.pallas_call(functools.partial(kernel, na, nx), out_shape=jax.ShapeDtyp...  74.3 us
    unnamed x7, local copies, waits for them, and re-layouts  3.08 us

profile of v8, /device:TPU:1, one launch (start us, length us, event | category | flops | bytes accessed | tf_op | source)
XLA Modules:
  0.0 77.4 jit_solution(2194907556274444647)
XLA Ops:
  0.0 0.0 copy-start.1
  0.0 0.7 copy-done.1
  0.7 0.0 copy-start
  0.7 1.1 %copy-done = bf16[512,768]{1,0:T(8,128)(2,1)S(1)} copy-done((bf16[512,768]{1,0:T(8,128)(2,1)S(1)}, bf16[512,768]{1,0:T(8,128)(2,1)}, u32[]{:S(2)}) %copy-start) | copy-done | bytes 786456
  1.8 0.0 copy-start.2
  1.8 0.7 copy-done.2
  2.5 74.3 %shard_map.37 = f32[1,512]{1,0:T(1,128)S(1)} custom-call(s32[1,512]{1,0:T(1,128)S(1)} %bitcast.4, s32[1,512]{1,0:T(1,128)S(1)} %bitcast.5, bf16[512,768]{1,0:T(8,128)(2,1)S(1)} %copy-done), custom_call_target="tpu_custom_call" | custom-call | tf_op jit(solution)/shard_map/pallas_call | solution.py:540
  76.8 0.6 copy.5
Async XLA Ops:
  0.0 0.7 copy-start.1
  0.7 1.1 %copy-start = (bf16[512,768]{1,0:T(8,128)(2,1)S(1)}, bf16[512,768]{1,0:T(8,128)(2,1)}, u32[]{:S(2)}) copy-start(bf16[512,768]{1,0:T(8,128)(2,1)} %emb_hbm.1) | copy-start | bytes 2359300
  1.8 0.7 copy-start.2
